TPU v7x, 128 devices: a whole 4x4x4 slice. The times are simulated.
128 devices in a mesh: fsdp: 4 (over y), ctx: 32 (over z, x, core).
Axes of the slice: x: 4, y: 4, z: 4, core: 2. Of those that a mesh axis runs over, the one named last changes fastest.
Arguments:
- tokens: bfloat16 [16384, 640], P(('fsdp', 'ctx')), may hold values from -6 to 6
- positions: int32 [16384], P(('fsdp', 'ctx')), may hold values from 0 to 12285, as said below
- w_query: bfloat16 [640, 1024], P('fsdp'), may hold values from -0.25 to 0.25
- w_key: bfloat16 [640, 256], P('fsdp'), may hold values from -0.25 to 0.25
- w_value: bfloat16 [640, 256], P('fsdp'), may hold values from -0.25 to 0.25
- w_out: bfloat16 [1024, 640], P('fsdp'), may hold values from -0.1875 to 0.1875
- w_gate: bfloat16 [640, 2048], P('fsdp'), may hold values from -0.25 to 0.25
- w_up: bfloat16 [640, 2048], P('fsdp'), may hold values from -0.25 to 0.25
- w_down: bfloat16 [2048, 640], P('fsdp'), may hold values from -0.125 to 0.125
- gain_in: bfloat16 [640], P('fsdp'), may hold values from 0.5 to 1.5
- gain_query: bfloat16 [256], P('fsdp'), may hold values from 0.099609375 to 1.8984375
- gain_key: bfloat16 [256], P('fsdp'), may hold values from 0.099609375 to 1.8984375
- gain_attn_post: bfloat16 [640], P('fsdp'), may hold values from 0.5 to 1.5
- gain_ffn_pre: bfloat16 [640], P('fsdp'), may hold values from 0.5 to 1.5
- gain_ffn_post: bfloat16 [640], P('fsdp'), may hold values from 0.5 to 1.5
- cotangent: bfloat16 [16384, 640], P(('fsdp', 'ctx')), may hold values from -6 to 6
Outputs:
- layer_out: bfloat16 [16384, 640], P(('fsdp', 'ctx'))
- input_grad: float32 [16384, 640], P(('fsdp', 'ctx'))
- w_query_grad: float32 [640, 1024], P('fsdp')
- w_key_grad: float32 [640, 256], P('fsdp')
- w_value_grad: float32 [640, 256], P('fsdp')
- w_out_grad: float32 [1024, 640], P('fsdp')
- w_gate_grad: float32 [640, 2048], P('fsdp')
- w_up_grad: float32 [640, 2048], P('fsdp')
- w_down_grad: float32 [2048, 640], P('fsdp')
- gain_in_grad: float32 [640], P('fsdp')
- gain_query_grad: float32 [256], P('fsdp')
- gain_key_grad: float32 [256], P('fsdp')
- gain_attn_post_grad: float32 [640], P('fsdp')
- gain_ffn_pre_grad: float32 [640], P('fsdp')
- gain_ffn_post_grad: float32 [640], P('fsdp')
Inputs may be any that keep to these rules, and one draw needn't show every extreme that they name: `positions`: within each sequence of 4096 tokens the ids start at 0 and rise by 1 to 3 from one token to the next; in one sequence they rise by 3 at every token.
All inputs are finite; a program needn't handle non-finite values.
Results may differ from a plain program's by a relative error of at most 0.033.
Values may be sent and summed in bfloat16 or wider, within the bound.
A program may use at most 128 MiB of HBM per device.

v0:
```python
import jax
import jax.numpy as jnp
from jax import lax
from jax.sharding import PartitionSpec as P

EPSILON = 1e-06
ROPE_BASE = 1000000.0
SCORE_SCALE = 0.0625
MASK_VALUE = -1e30


def side_by_side(arrays, axis, dim, along):
    widths = [a.shape[along] for a in arrays]
    both = jnp.concatenate(arrays, axis=along)
    whole = lax.all_gather(both, axis, axis=dim, tiled=True)
    return tuple(jnp.split(whole, [sum(widths[:k]) for k in range(1, len(widths))], axis=along))


def sent_together(arrays, axis, dim, along):
    widths = [a.shape[along] for a in arrays]
    both = jnp.concatenate(arrays, axis=along)
    whole = lax.psum_scatter(both, axis, scatter_dimension=dim, tiled=True)
    return tuple(jnp.split(whole, [sum(widths[:k]) for k in range(1, len(widths))], axis=along))


def rms_scale(values, gain_vector):
    return (
        values
        * lax.rsqrt(jnp.mean(values * values, axis=-1, keepdims=True) + EPSILON)
        * gain_vector
    )


def rotate(values, cosine, sine_table):
    half_size = values.shape[-1] // 2
    first_half = values[..., :half_size]
    second_half = values[..., half_size:]
    return jnp.concatenate(
        [
            first_half * cosine - second_half * sine_table,
            second_half * cosine + first_half * sine_table,
        ],
        axis=-1,
    )


def rope_tables(positions, head_dim):
    exponents = jnp.arange(0, head_dim, 2, dtype=jnp.float32) / head_dim
    inverse = 1.0 / ROPE_BASE**exponents
    angles = positions.astype(jnp.float32)[:, None] * inverse[None, :]
    return (jnp.cos(angles), jnp.sin(angles))


def gelu_product(gate_value, upward):
    return jax.nn.gelu(gate_value, approximate=True) * upward


def transpose_dot(left_side, right_side):
    return lax.dot_general(
        left_side, right_side, (((0,), (0,)), ((), ())), preferred_element_type=jnp.float32
    )


def dot_back(left_side, right_side):
    return lax.dot_general(
        left_side, right_side, (((1,), (1,)), ((), ())), preferred_element_type=jnp.float32
    )


def local(
    tokens,
    positions,
    w_query,
    w_key,
    w_value,
    w_out,
    w_gate,
    w_up,
    w_down,
    gain_in,
    gain_query,
    gain_key,
    gain_attn_post,
    gain_ffn_pre,
    gain_ffn_post,
    cotangent,
):
    query_full, key_full, value_full, out_full, norm_in, norm_query, norm_key, attn_post = (
        *side_by_side((w_query, w_key, w_value), "fsdp", 0, 1),
        lax.all_gather(w_out, "fsdp", axis=0, tiled=True),
        lax.all_gather(gain_in, "fsdp", axis=0, tiled=True),
        lax.all_gather(gain_query, "fsdp", axis=0, tiled=True),
        lax.all_gather(gain_key, "fsdp", axis=0, tiled=True),
        lax.all_gather(gain_attn_post, "fsdp", axis=0, tiled=True),
    )
    gate_full, up_full, down_full, ffn_pre, ffn_post = (
        *side_by_side((w_gate, w_up), "fsdp", 0, 1),
        lax.all_gather(w_down, "fsdp", axis=0, tiled=True),
        lax.all_gather(gain_ffn_pre, "fsdp", axis=0, tiled=True),
        lax.all_gather(gain_ffn_post, "fsdp", axis=0, tiled=True),
    )
    tok_count = tokens.shape[0]
    head_dim = key_full.shape[1]
    heads_count = query_full.shape[1] // head_dim
    row_count = tok_count * heads_count
    ctx_size = lax.axis_size("ctx")
    ctx_index = lax.axis_index("ctx")
    own_start = ctx_index * tok_count
    last_row = own_start + tok_count - 1
    inputs = tokens.astype(jnp.float32)
    normed, input_back = jax.vjp(rms_scale, inputs, norm_in.astype(jnp.float32))
    normed_low = normed.astype(jnp.bfloat16)
    query_raw = jnp.dot(normed_low, query_full, preferred_element_type=jnp.float32)
    key_raw = jnp.dot(normed_low, key_full, preferred_element_type=jnp.float32)
    value_low = jnp.dot(normed_low, value_full, preferred_element_type=jnp.float32).astype(
        jnp.bfloat16
    )
    cosine, sine_table = rope_tables(positions, head_dim)

    def shape_query(raw_query, gain_vector):
        normed_heads = rms_scale(raw_query.reshape(tok_count, heads_count, head_dim), gain_vector)
        return rotate(normed_heads, cosine[:, None, :], sine_table[:, None, :])

    def shape_key(raw_key, gain_vector):
        return rotate(rms_scale(raw_key, gain_vector), cosine, sine_table)

    query_rot, query_back = jax.vjp(shape_query, query_raw, norm_query.astype(jnp.float32))
    key_rot, key_back = jax.vjp(shape_key, key_raw, norm_key.astype(jnp.float32))
    query_low = query_rot.reshape(row_count, head_dim).astype(jnp.bfloat16)
    key_low = key_rot.astype(jnp.bfloat16)
    row_pos = own_start + jnp.arange(row_count, dtype=jnp.int32) // heads_count

    def masked_scores(key_block, start):
        key_pos = start + jnp.arange(key_block.shape[0], dtype=jnp.int32)
        raw_scores = dot_back(query_low, key_block) * SCORE_SCALE
        return jnp.where(key_pos[None, :] <= row_pos[:, None], raw_scores, MASK_VALUE)

    def lse_block(carry, key_block, start):
        row_max, row_sum = carry
        scores = masked_scores(key_block, start)
        new_max = jnp.maximum(row_max, jnp.max(scores, axis=1))
        row_sum = row_sum * jnp.exp(row_max - new_max) + jnp.sum(
            jnp.exp(scores - new_max[:, None]), axis=1
        )
        return (new_max, row_sum)

    def out_block(total, key_block, value_block, start):
        probs = jnp.exp(masked_scores(key_block, start) - row_lse[:, None]).astype(jnp.bfloat16)
        return total + jnp.dot(probs, value_block, preferred_element_type=jnp.float32)

    def grad_block(carry, key_block, value_block, start):
        query_grad, block_key_grad, block_value_grad = carry
        probs = jnp.exp(masked_scores(key_block, start) - row_lse[:, None])
        prob_grad = dot_back(out_grad_low, value_block)
        score_grad = (probs * (prob_grad - delta[:, None])).astype(jnp.bfloat16)
        query_grad = (
            query_grad
            + jnp.dot(score_grad, key_block, preferred_element_type=jnp.float32) * SCORE_SCALE
        )
        block_key_grad = transpose_dot(score_grad, query_low) * SCORE_SCALE
        block_value_grad = transpose_dot(probs.astype(jnp.bfloat16), out_grad_low)
        return (query_grad, block_key_grad, block_value_grad)

    def unchanged(inner):
        return inner

    lse_init = (
        jnp.full((row_count,), MASK_VALUE, jnp.float32),
        jnp.zeros((row_count,), jnp.float32),
    )
    out_init = jnp.zeros((row_count, head_dim), jnp.float32)
    key_all, value_all = side_by_side((key_low, value_low), "ctx", 0, 1)
    block_span = 4 * tok_count
    block_total = ctx_size // 4

    def lse_turn(block_index, state):
        start = block_index * block_span
        key_block = lax.dynamic_slice_in_dim(key_all, start, block_span, 0)

        def lse_active(inner):
            return lse_block(inner, key_block, start)

        return lax.cond(start <= last_row, lse_active, unchanged, state)

    lse_state = lax.fori_loop(0, block_total, lse_turn, lse_init)
    row_lse = lse_state[0] + jnp.log(lse_state[1])

    def out_turn(block_index, state):
        start = block_index * block_span
        key_block = lax.dynamic_slice_in_dim(key_all, start, block_span, 0)
        value_block = lax.dynamic_slice_in_dim(value_all, start, block_span, 0)

        def out_active(inner):
            return out_block(inner, key_block, value_block, start)

        return lax.cond(start <= last_row, out_active, unchanged, state)

    attended = lax.fori_loop(0, block_total, out_turn, out_init)
    attn_low = attended.reshape(tok_count, heads_count * head_dim).astype(jnp.bfloat16)
    proj = jnp.dot(attn_low, out_full, preferred_element_type=jnp.float32)
    post_attn, post_attn_back = jax.vjp(rms_scale, proj, attn_post.astype(jnp.float32))
    hidden = inputs + post_attn
    ffn_in, ffn_in_back = jax.vjp(rms_scale, hidden, ffn_pre.astype(jnp.float32))
    ffn_low = ffn_in.astype(jnp.bfloat16)
    gate_value = jnp.dot(ffn_low, gate_full, preferred_element_type=jnp.float32)
    up_value = jnp.dot(ffn_low, up_full, preferred_element_type=jnp.float32)
    mixed, mixed_back = jax.vjp(gelu_product, gate_value, up_value)
    mixed_low = mixed.astype(jnp.bfloat16)
    down_value = jnp.dot(mixed_low, down_full, preferred_element_type=jnp.float32)
    post_ffn, post_ffn_back = jax.vjp(rms_scale, down_value, ffn_post.astype(jnp.float32))
    layer_out = (hidden + post_ffn).astype(jnp.bfloat16)
    out_grad = cotangent.astype(jnp.float32)
    down_grad, ffn_post_grad = post_ffn_back(out_grad)
    down_low = down_grad.astype(jnp.bfloat16)
    down_wgrad = transpose_dot(mixed_low, down_low)
    mixed_grad = dot_back(down_low, down_full)
    gate_grad, up_grad = mixed_back(mixed_grad)
    gate_low = gate_grad.astype(jnp.bfloat16)
    up_low = up_grad.astype(jnp.bfloat16)
    gate_wgrad = transpose_dot(ffn_low, gate_low)
    up_wgrad = transpose_dot(ffn_low, up_low)
    ffn_in_grad = dot_back(gate_low, gate_full) + dot_back(up_low, up_full)
    hidden_part, ffn_pre_grad = ffn_in_back(ffn_in_grad)
    hidden_grad = out_grad + hidden_part
    proj_grad, attn_post_grad = post_attn_back(hidden_grad)
    proj_low = proj_grad.astype(jnp.bfloat16)
    out_wgrad = transpose_dot(attn_low, proj_low)
    out_grad_low = dot_back(proj_low, out_full).astype(jnp.bfloat16).reshape(row_count, head_dim)
    delta = jnp.sum(out_grad_low.astype(jnp.float32) * attended, axis=1)
    seq_keys = key_all.shape[0]

    def grad_turn(block_index, state):
        start = block_index * block_span
        key_block = lax.dynamic_slice_in_dim(key_all, start, block_span, 0)
        value_block = lax.dynamic_slice_in_dim(value_all, start, block_span, 0)

        def grad_active(inner):
            zero_block = jnp.zeros((block_span, head_dim), jnp.float32)
            new_query, block_key, block_value = grad_block(
                (inner[0], zero_block, zero_block), key_block, value_block, start
            )
            return (
                new_query,
                lax.dynamic_update_slice_in_dim(inner[1], block_key, start, 0),
                lax.dynamic_update_slice_in_dim(inner[2], block_value, start, 0),
            )

        return lax.cond(start <= last_row, grad_active, unchanged, state)

    empty_all = jnp.zeros((seq_keys, head_dim), jnp.float32)
    query_grad, key_grads, value_grads = lax.fori_loop(
        0, block_total, grad_turn, (out_init, empty_all, empty_all)
    )
    key_grad_total, value_grad_total = tuple(
        (
            part.astype(jnp.float32)
            for part in sent_together(
                (key_grads.astype(jnp.bfloat16), value_grads.astype(jnp.bfloat16)), "ctx", 0, 1
            )
        )
    )
    value_grad_low = value_grad_total.astype(jnp.bfloat16)
    query_raw_grad, query_norm_grad = query_back(
        query_grad.reshape(tok_count, heads_count, head_dim)
    )
    key_raw_grad, key_norm_grad = key_back(key_grad_total)
    query_raw_low = query_raw_grad.astype(jnp.bfloat16)
    key_raw_low = key_raw_grad.astype(jnp.bfloat16)
    query_wgrad = transpose_dot(normed_low, query_raw_low)
    key_wgrad = transpose_dot(normed_low, key_raw_low)
    value_wgrad = transpose_dot(normed_low, value_grad_low)
    normed_grad = (
        dot_back(query_raw_low, query_full)
        + dot_back(key_raw_low, key_full)
        + dot_back(value_grad_low, value_full)
    )
    input_part, norm_in_grad = input_back(normed_grad)
    input_grad = hidden_grad + input_part
    attn_shares = (
        *tuple(
            (
                part.astype(jnp.float32)
                for part in sent_together(
                    (
                        query_wgrad.astype(jnp.bfloat16),
                        key_wgrad.astype(jnp.bfloat16),
                        value_wgrad.astype(jnp.bfloat16),
                    ),
                    "fsdp",
                    0,
                    1,
                )
            )
        ),
        lax.psum_scatter(
            out_wgrad.astype(jnp.bfloat16), "fsdp", scatter_dimension=0, tiled=True
        ).astype(jnp.float32),
        lax.psum_scatter(
            norm_in_grad.astype(jnp.bfloat16), "fsdp", scatter_dimension=0, tiled=True
        ).astype(jnp.float32),
        lax.psum_scatter(
            query_norm_grad.astype(jnp.bfloat16), "fsdp", scatter_dimension=0, tiled=True
        ).astype(jnp.float32),
        lax.psum_scatter(
            key_norm_grad.astype(jnp.bfloat16), "fsdp", scatter_dimension=0, tiled=True
        ).astype(jnp.float32),
        lax.psum_scatter(
            attn_post_grad.astype(jnp.bfloat16), "fsdp", scatter_dimension=0, tiled=True
        ).astype(jnp.float32),
    )
    ffn_shares = (
        *tuple(
            (
                part.astype(jnp.float32)
                for part in sent_together(
                    (gate_wgrad.astype(jnp.bfloat16), up_wgrad.astype(jnp.bfloat16)), "fsdp", 0, 1
                )
            )
        ),
        lax.psum_scatter(
            down_wgrad.astype(jnp.bfloat16), "fsdp", scatter_dimension=0, tiled=True
        ).astype(jnp.float32),
        lax.psum_scatter(
            ffn_pre_grad.astype(jnp.bfloat16), "fsdp", scatter_dimension=0, tiled=True
        ).astype(jnp.float32),
        lax.psum_scatter(
            ffn_post_grad.astype(jnp.bfloat16), "fsdp", scatter_dimension=0, tiled=True
        ).astype(jnp.float32),
    )
    totals = (
        lax.psum(attn_shares[0].astype(jnp.bfloat16), "ctx").astype(jnp.float32),
        lax.psum(attn_shares[1].astype(jnp.bfloat16), "ctx").astype(jnp.float32),
        lax.psum(attn_shares[2].astype(jnp.bfloat16), "ctx").astype(jnp.float32),
        lax.psum(attn_shares[3].astype(jnp.bfloat16), "ctx").astype(jnp.float32),
        lax.psum(ffn_shares[0].astype(jnp.bfloat16), "ctx").astype(jnp.float32),
        lax.psum(ffn_shares[1].astype(jnp.bfloat16), "ctx").astype(jnp.float32),
        lax.psum(ffn_shares[2].astype(jnp.bfloat16), "ctx").astype(jnp.float32),
        lax.psum(attn_shares[4].astype(jnp.bfloat16), "ctx").astype(jnp.float32),
        lax.psum(attn_shares[5].astype(jnp.bfloat16), "ctx").astype(jnp.float32),
        lax.psum(attn_shares[6].astype(jnp.bfloat16), "ctx").astype(jnp.float32),
        lax.psum(attn_shares[7].astype(jnp.bfloat16), "ctx").astype(jnp.float32),
        lax.psum(ffn_shares[3].astype(jnp.bfloat16), "ctx").astype(jnp.float32),
        lax.psum(ffn_shares[4].astype(jnp.bfloat16), "ctx").astype(jnp.float32),
    )
    return (
        layer_out,
        input_grad,
        totals[0],
        totals[1],
        totals[2],
        totals[3],
        totals[4],
        totals[5],
        totals[6],
        totals[7],
        totals[8],
        totals[9],
        totals[10],
        totals[11],
        totals[12],
    )


def solution(mesh):
    in_specs = (
        P(("fsdp", "ctx"), None),
        P(("fsdp", "ctx")),
        P("fsdp", None),
        P("fsdp", None),
        P("fsdp", None),
        P("fsdp", None),
        P("fsdp", None),
        P("fsdp", None),
        P("fsdp", None),
        P("fsdp"),
        P("fsdp"),
        P("fsdp"),
        P("fsdp"),
        P("fsdp"),
        P("fsdp"),
        P(("fsdp", "ctx"), None),
    )
    out_specs = (
        P(("fsdp", "ctx"), None),
        P(("fsdp", "ctx"), None),
        P("fsdp", None),
        P("fsdp", None),
        P("fsdp", None),
        P("fsdp", None),
        P("fsdp", None),
        P("fsdp", None),
        P("fsdp", None),
        P("fsdp"),
        P("fsdp"),
        P("fsdp"),
        P("fsdp"),
        P("fsdp"),
        P("fsdp"),
    )
    return jax.shard_map(local, mesh=mesh, in_specs=in_specs, out_specs=out_specs, check_vma=False)
```

profile of v0, /device:TPU:1, one launch (start us, length us, event | category | flops | bytes accessed | tf_op | source)
XLA Modules:
  0.0 654.2 jit_solution(14944994057698102678)
XLA Ops:
  7.3 2.0 pad_maximum_fusion.4
  17.0 9.8 %all-reduce.19 = (bf16[640]{0:T(1024)(128)(2,1)S(1)}, bf16[256]{0:T(256)(128)(2,1)S(1)}, bf16[256]{0:T(256)(128)(2,1)S(1)}, bf16[640]{0:T(1024)(128)(2,1)S(1)}, ...) all-reduce(bf16[640]{0:T(1024)(128)(2,1)S(1)} %dynamic-update-slice, ...), channel_id=1, replica_groups=mesh['fsdp'=4,'ctx'=32] {'fsdp'}, use_global_device_ids=true, to_apply=%add.4 | all-reduce | flops 3072 | bytes 12288
  28.5 14.9 %all-gather.6.cloned.1.call-done = bf16[640,1536]{1,0:T(8,128)(2,1)} async-done(((bf16[160,1536]{1,0:T(8,128)(2,1)}), bf16[640,1536]{1,0:T(8,128)(2,1)}) %all-gather.6.cloned.1.call-update) | async-done | bytes 1966096 | tf_op jit(solution)/shard_map/all_gather | solution.py:15
  54.1 40.7 %all-gather.8.cloned.1.call-done = bf16[4096,512]{1,0:T(8,128)(2,1)} async-done(((bf16[128,512]{1,0:T(8,128)(2,1)}), bf16[4096,512]{1,0:T(8,128)(2,1)}) %all-gather.8.cloned.1.call-update) | async-done | bytes 4194320 | tf_op jit(solution)/shard_map/all_gather | solution.py:15
  94.7 3.8 fusion.123
  100.5 3.1 while.52
  100.5 2.7 conditional.10
  100.5 2.7 fusion.18
  106.6 12.5 %all-gather.10.cloned.1.call-done = bf16[1024,640]{1,0:T(8,128)(2,1)} async-done(((bf16[256,640]{1,0:T(8,128)(2,1)}), bf16[1024,640]{1,0:T(8,128)(2,1)}) %all-gather.10.cloned.1.call-update) | async-done | bytes 1310736 | tf_op jit(solution)/shard_map/all_gather | solution.py:90
  119.1 1.9 multiply_reduce_fusion.10
  122.4 57.5 %all-gather.12.cloned.1.call-done = bf16[640,4096]{1,0:T(8,128)(2,1)} async-done(((bf16[160,4096]{1,0:T(8,128)(2,1)}), bf16[640,4096]{1,0:T(8,128)(2,1)}) %all-gather.12.cloned.1.call-update) | async-done | bytes 5242896 | tf_op jit(solution)/shard_map/all_gather | solution.py:15
  179.9 2.3 fusion.58
  183.2 3.5 multiply_convert_fusion.1
  186.7 30.5 %all-gather.14.cloned.1.call-done = bf16[2048,640]{1,0:T(8,128)(2,1)} async-done(((bf16[512,640]{1,0:T(8,128)(2,1)}), bf16[2048,640]{1,0:T(8,128)(2,1)}) %all-gather.14.cloned.1.call-update) | async-done | bytes 2621456 | tf_op jit(solution)/shard_map/all_gather | solution.py:98
  217.2 2.6 multiply_reduce_fusion.8
  221.4 3.1 fusion.73
  232.4 6.5 while.53
  232.4 6.1 conditional.11
  238.9 4.5 pad_maximum_fusion.1
  246.6 119.0 %reduce-scatter.6.cloned.1.call-done = bf16[128,512]{1,0:T(8,128)(2,1)} async-done(((bf16[4096,512]{1,0:T(8,128)(2,1)}), bf16[128,512]{1,0:T(8,128)(2,1)}) %reduce-scatter.6.cloned.1.call-update) | async-done | bytes 131088 | tf_op jit(solution)/shard_map/reduce_scatter | solution.py:22
  373.3 2.7 pad_maximum_fusion
  378.7 2.4 convolution_convert_fusion
  381.2 19.1 %reduce-scatter.8.cloned.1.call-done = bf16[160,1536]{1,0:T(8,128)(2,1)} async-done(((bf16[640,1536]{1,0:T(8,128)(2,1)}), bf16[160,1536]{1,0:T(8,128)(2,1)}) %reduce-scatter.8.cloned.1.call-update) | async-done | bytes 491536 | tf_op jit(solution)/shard_map/reduce_scatter | solution.py:22
  403.5 54.4 %reduce-scatter.12.cloned.1.call-done = bf16[160,4096]{1,0:T(8,128)(2,1)} async-done(((bf16[640,4096]{1,0:T(8,128)(2,1)}), bf16[160,4096]{1,0:T(8,128)(2,1)}) %reduce-scatter.12.cloned.1.call-update) | async-done | bytes 1310736 | tf_op jit(solution)/shard_map/reduce_scatter | solution.py:22
  457.9 2.5 fusion.124
  460.4 23.6 %reduce-scatter.10.cloned.1.call-done = bf16[256,640]{1,0:T(8,128)(2,1)} async-done(((bf16[1024,640]{1,0:T(8,128)(2,1)}), bf16[256,640]{1,0:T(8,128)(2,1)}) %reduce-scatter.10.cloned.1.call-update) | async-done | bytes 327696 | tf_op jit(solution)/shard_map/reduce_scatter | solution.py:295
  484.0 37.4 %reduce-scatter.14.cloned.1.call-done = bf16[512,640]{1,0:T(8,128)(2,1)} async-done(((bf16[2048,640]{1,0:T(8,128)(2,1)}), bf16[512,640]{1,0:T(8,128)(2,1)}) %reduce-scatter.14.cloned.1.call-update) | async-done | bytes 655376 | tf_op jit(solution)/shard_map/reduce_scatter | solution.py:320
  522.8 1.9 fusion.63
  527.3 6.8 %all-reduce.18 = (bf16[640]{0:T(1024)(128)(2,1)S(1)}, bf16[256]{0:T(256)(128)(2,1)S(1)}, bf16[256]{0:T(256)(128)(2,1)S(1)}, bf16[640]{0:T(1024)(128)(2,1)S(1)}, ...) all-reduce(bf16[640]{0:T(1024)(128)(2,1)S(1)} %get-tuple-element.10, ...), channel_id=7, replica_groups=mesh['fsdp'=4,'ctx'=32] {'fsdp'}, use_global_device_ids=true, to_apply=%region_40.41.clone | all-reduce | flops 3072 | bytes 12288
  534.6 64.9 %all-reduce.16 = (bf16[160]{0:T(256)(128)(2,1)S(1)}, bf16[64]{0:T(256)(128)(2,1)S(1)}, bf16[64]{0:T(256)(128)(2,1)S(1)}, bf16[160]{0:T(256)(128)(2,1)S(1)}, bf16...) all-reduce(bf16[160]{0:T(256)(128)(2,1)S(1)} %dynamic-slice.7, ...), channel_id=1, replica_groups=mesh['fsdp'=4,'ctx'=32] {'ctx'}, use_global_device_ids=true, to_apply=%region_41.42 | all-reduce | flops 768 | bytes 3072 | tf_op jit(solution)/shard_map/psum | solution.py:338
  603.6 33.5 %all-reduce.22.cloned.1.call-done = (bf16[160,1024]{1,0:T(8,128)(2,1)}, bf16[160,256]{1,0:T(8,128)(2,1)}, bf16[160,256]{1,0:T(8,128)(2,1)}, bf16[256,640]{1,0:T(...) async-done(((bf16[160,1024]{1,0:T(8,128)(2,1)}, bf16[160,256]{1,0:T(8,128)(2,1)}, bf16[160,256]{1,0:T(8,128)(2,1)}, ...) | async-done | bytes 2785296 | tf_op jit(solution)/shard_map/psum | solution.py:331
  637.1 2.0 convert_element_type.266
  (355 shorter events, 75.1 us)
Async XLA Ops:
  7.2 38.8 %copy-start = (bf16[128,640]{1,0:T(8,128)(2,1)S(1)}, bf16[128,640]{1,0:T(8,128)(2,1)}, u32[]{:S(2)}) copy-start(bf16[128,640]{1,0:T(8,128)(2,1)} %param.28) | copy-start | bytes 491524
  7.2 41.5 %copy-start.19 = (bf16[160,2048]{1,0:T(8,128)(2,1)S(1)}, bf16[160,2048]{1,0:T(8,128)(2,1)}, u32[]{:S(2)}) copy-start(bf16[160,2048]{1,0:T(8,128)(2,1)} %param.35) | copy-start | bytes 1966084
  7.2 41.5 %copy-start.20 = (bf16[160,2048]{1,0:T(8,128)(2,1)S(1)}, bf16[160,2048]{1,0:T(8,128)(2,1)}, u32[]{:S(2)}) copy-start(bf16[160,2048]{1,0:T(8,128)(2,1)} %param.34) | copy-start | bytes 1966084
  7.2 36.2 %all-gather.6.cloned.1.call-start = ((), (), s32[]{:S(2)}) async-start(), calls=%async_computation.5 | async-start | bytes 2457600 | tf_op jit(solution)/shard_map/all_gather | solution.py:15
  9.3 85.5 %all-gather.8.cloned.1.call-start = ((), (), s32[]{:S(2)}) async-start(), calls=%async_computation.6 | async-start | bytes 4325376 | tf_op jit(solution)/shard_map/all_gather | solution.py:15
  27.4 18.1 %copy-start.49 = (f32[128]{0:T(128)}, f32[128]{0:T(128)S(1)}, u32[]{:S(2)}) copy-start(f32[128]{0:T(128)S(1)} %convert_element_type.238) | copy-start | bytes 1540
  27.4 17.4 %copy-start.39 = (f32[256]{0:T(256)}, f32[256]{0:T(256)S(1)}, u32[]{:S(2)}) copy-start(f32[256]{0:T(256)S(1)} %convert_element_type.237) | copy-start | bytes 3076
  27.4 18.1 %copy-start.51 = (f32[128]{0:T(128)}, f32[128]{0:T(128)S(1)}, u32[]{:S(2)}) copy-start(f32[128]{0:T(128)S(1)} %negate_power_fusion) | copy-start | bytes 1540
  28.5 17.1 %copy-start.59 = (f32[128]{0:T(128)}, f32[128]{0:T(128)S(1)}, u32[]{:S(2)}) copy-start(f32[128]{0:T(128)S(1)} %fusion.86) | copy-start | bytes 1540
  28.5 22.3 %copy-start.37 = (f32[128]{0:T(128)}, f32[128]{0:T(128)S(1)}, u32[]{:S(2)}) copy-start(f32[128]{0:T(128)S(1)} %fusion.111) | copy-start | bytes 1540
  46.0 7.8 %copy-start.26 = (f32[128,128]{1,0:T(8,128)}, f32[128,128]{1,0:T(8,128)S(1)}, u32[]{:S(2)}) copy-start(f32[128,128]{1,0:T(8,128)S(1)} %get-tuple-element.1126) | copy-start | bytes 196612
  48.0 71.1 %all-gather.10.cloned.1.call-start = ((), (), s32[]{:S(2)}) async-start(), calls=%async_computation.7 | async-start | bytes 1638400 | tf_op jit(solution)/shard_map/all_gather | solution.py:90
  48.7 131.2 %all-gather.12.cloned.1.call-start = ((), (), s32[]{:S(2)}) async-start(), calls=%async_computation.8 | async-start | bytes 6553600 | tf_op jit(solution)/shard_map/all_gather | solution.py:15
  49.9 167.3 %all-gather.14.cloned.1.call-start = ((), (), s32[]{:S(2)}) async-start(), calls=%async_computation.9 | async-start | bytes 3276800 | tf_op jit(solution)/shard_map/all_gather | solution.py:98
  50.5 315.0 %reduce-scatter.6.cloned.1.call-start = ((), (), s32[]{:S(2)}) async-start(), calls=%async_computation.10 | async-start | bytes 4325376 | tf_op jit(solution)/shard_map/reduce_scatter | solution.py:22
  104.2 18.2 %copy-start.1 = (bf16[4096,256]{1,0:T(8,128)(2,1)}, bf16[4096,256]{1,0:T(8,128)(2,1)S(1)}, u32[]{:S(2)}) copy-start(bf16[4096,256]{1,0:T(8,128)(2,1)S(1)} %get-tuple-element.1467) | copy-start | bytes 6291460
  186.7 34.6 %copy-start.8 = (bf16[128,2048]{1,0:T(8,128)(2,1)}, bf16[128,2048]{1,0:T(8,128)(2,1)S(1)}, u32[]{:S(2)}) copy-start(bf16[128,2048]{1,0:T(8,128)(2,1)S(1)} %get-tuple-element.1136) | copy-start | bytes 1572868
  186.7 33.0 %copy-start.10 = (bf16[128,640]{1,0:T(8,128)(2,1)S(1)}, bf16[128,640]{1,0:T(8,128)(2,1)}, u32[]{:S(2)}) copy-start(bf16[128,640]{1,0:T(8,128)(2,1)} %param.43) | copy-start | bytes 491524
  186.7 33.8 %copy-start.4 = (f32[128,640]{1,0:T(8,128)S(1)}, f32[128,640]{1,0:T(8,128)}, u32[]{:S(2)}) copy-start(f32[128,640]{1,0:T(8,128)} %copy-done.3) | copy-start | bytes 983044
  243.4 156.8 %reduce-scatter.8.cloned.1.call-start = ((), (), s32[]{:S(2)}) async-start(), calls=%async_computation.11 | async-start | bytes 2457600 | tf_op jit(solution)/shard_map/reduce_scatter | solution.py:22
  245.3 121.1 %copy-start.50 = (f32[128]{0:T(128)S(1)}, f32[128]{0:T(128)}, u32[]{:S(2)}) copy-start(f32[128]{0:T(128)} %copy-done.49) | copy-start | bytes 1540
  245.3 121.1 %copy-start.52 = (f32[128]{0:T(128)S(1)}, f32[128]{0:T(128)}, u32[]{:S(2)}) copy-start(f32[128]{0:T(128)} %copy-done.51) | copy-start | bytes 1540
  245.5 121.2 %copy-start.14 = (f32[128,256]{1,0:T(8,128)S(1)}, f32[128,256]{1,0:T(8,128)}, u32[]{:S(2)}) copy-start(f32[128,256]{1,0:T(8,128)} %copy-done.13) | copy-start | bytes 393220
  245.5 121.2 %copy-start.40 = (f32[256]{0:T(256)S(1)}, f32[256]{0:T(256)}, u32[]{:S(2)}) copy-start(f32[256]{0:T(256)} %copy-done.39) | copy-start | bytes 3076
  245.5 121.2 %copy-start.45 = (f32[128]{0:T(128)S(1)}, f32[128]{0:T(128)}, u32[]{:S(2)}) copy-start(f32[128]{0:T(128)} %copy-done.44) | copy-start | bytes 1540
  245.6 121.9 %copy-start.66 = (f32[128]{0:T(128)S(1)}, f32[128]{0:T(128)}, u32[]{:S(2)}) copy-start(f32[128]{0:T(128)} %copy-done.65) | copy-start | bytes 1540
  370.6 87.4 %reduce-scatter.12.cloned.1.call-start = ((), (), s32[]{:S(2)}) async-start(), calls=%async_computation.13 | async-start | bytes 6553600 | tf_op jit(solution)/shard_map/reduce_scatter | solution.py:22
  376.1 107.9 %reduce-scatter.10.cloned.1.call-start = ((), (), s32[]{:S(2)}) async-start(), calls=%async_computation.12 | async-start | bytes 1638400 | tf_op jit(solution)/shard_map/reduce_scatter | solution.py:295
  378.6 142.8 %reduce-scatter.14.cloned.1.call-start = ((), (), s32[]{:S(2)}) async-start(), calls=%async_computation.14 | async-start | bytes 3276800 | tf_op jit(solution)/shard_map/reduce_scatter | solution.py:320
  381.1 256.0 %all-reduce.22.cloned.1.call-start = ((), (), s32[]{:S(2)}) async-start(), calls=%async_computation.15 | async-start | bytes 5570560 | tf_op jit(solution)/shard_map/psum | solution.py:331
  522.8 79.9 %copy-start.60 = (f32[128]{0:T(128)S(1)}, f32[128]{0:T(128)}, u32[]{:S(2)}) copy-start(f32[128]{0:T(128)} %copy-done.59) | copy-start | bytes 1540
  637.1 8.2 %copy-start.24 = (bf16[160,2048]{1,0:T(8,128)(2,1)S(1)}, bf16[160,2048]{1,0:T(8,128)(2,1)}, u32[]{:S(2)}) copy-start(bf16[160,2048]{1,0:T(8,128)(2,1)} %get-tuple-element.1083) | copy-start | bytes 1966084
  (48 other events, 106.4 us)
Sparse Core Ops, SparseCore 0:
  10.3 33.1 all-gather.5
  48.1 46.6 all-gather.7
  96.4 22.6 all-gather.9
  121.2 58.7 all-gather.11
  181.4 35.7 all-gather.13
  243.5 121.9 reduce-scatter.5
  370.7 29.4 reduce-scatter.7
  402.8 55.1 reduce-scatter.11
  461.1 22.8 reduce-scatter.9
  486.4 34.9 reduce-scatter.13
  527.0 110.0 all-reduce.21
where the time goes:
time: 656 us; the launch traced here: 654 us
  waiting for transfers between devices  444 us (68%)
  blocking collectives  81.4 us (12%)
  matrix products  42.2 us (6%)
  other arithmetic  37.5 us (6%)
  local copies, waits for them, and re-layouts  29 us (4%)
  between operations  17.6 us (3%)
    reduce_scatter x3, waiting for transfers between devices, sent_together(): whole = lax.psum_scatter(both, axis, scatter_dimension=dim, tiled=True)  192 us
    all_gather x3, waiting for transfers between devices, side_by_side(): whole = lax.all_gather(both, axis, axis=dim, tiled=True)  113 us
    psum x1, blocking collectives, local(): lax.psum(attn_shares[4].astype(jnp.bfloat16), 'ctx').astype(jnp.float32)  64.9 us
    reduce_scatter x1, waiting for transfers between devices, local(): lax.psum_scatter(down_wgrad.astype(jnp.bfloat16), 'fsdp', scatter_dimensi...  37.4 us
    psum x1, waiting for transfers between devices, local(): lax.psum(attn_shares[0].astype(jnp.bfloat16), 'ctx').astype(jnp.float32)  33.5 us
    all_gather x1, waiting for transfers between devices, local(): lax.all_gather(w_down, 'fsdp', axis=0, tiled=True)  30.5 us
    reduce_scatter x1, waiting for transfers between devices, local(): lax.psum_scatter(out_wgrad.astype(jnp.bfloat16), 'fsdp', scatter_dimensio...  23.6 us
    unnamed x2, blocking collectives  16.5 us
  transfers between devices with their start and end apart: 11, of which 11 were waited for; matrix products, arithmetic and copies ran while one was open for 9% of the time, Pallas kernels for 0%

commit v1 on v0

v1 whole, which is shorter than its diff:
```python
import functools

import jax
import jax.numpy as jnp
from jax import lax
from jax.experimental import pallas as pl
from jax.experimental.pallas import tpu as pltpu
from jax.sharding import PartitionSpec as P

EPS = 1e-06
ROPE_BASE = 1000000.0
BF = jnp.bfloat16
F32 = jnp.float32
MESH = pl.DeviceIdType.MESH
VMEM = pltpu.VMEM
VSPEC = pl.BlockSpec(memory_space=pltpu.VMEM)
ANYSPEC = pl.BlockSpec(memory_space=pl.ANY)
VMEM_LIMIT = 60 * 1024 * 1024
C_ROOT = 0.7978845608028654
C_CUBE = 0.044715

PART_UNITS = (96, 128, 128)
PART_OFF = (0, 1536, 3584)
ROWS = 5632
OFF_Q, OFF_K, OFF_V, OFF_G, OFF_U, OFF_O, OFF_D, OFF_GAIN = 0, 640, 800, 960, 2240, 3520, 4160, 5440
GAIN_ROWS = 16


class Net:
    def __init__(self, send_sem, recv_sem):
        me = lax.axis_index("ctx")
        self.y = lax.axis_index("fsdp")
        self.c = lax.rem(me, 2)
        self.x = lax.rem(lax.div(me, 2), 4)
        self.z = lax.div(me, 8)
        self.send_sem, self.recv_sem = send_sem, recv_sem
        self.used = 0
        self.sent = []

    def pos(self, axis):
        return {"x": self.x, "y": self.y, "z": self.z, "c": self.c}[axis]

    def at(self, axis, step):
        return lax.rem(self.pos(axis) + (step + 4), 4)

    def dev(self, axis, step):
        x, y, z, c = self.x, self.y, self.z, self.c
        if axis == "x":
            x = self.at("x", step)
        elif axis == "y":
            y = self.at("y", step)
        elif axis == "z":
            z = self.at("z", step)
        else:
            c = 1 - c
        return {"fsdp": y, "ctx": z * 8 + x * 2 + c}

    def copy(self, src, dst, axis, step=1):
        k = self.used
        self.used += 1
        cp = pltpu.make_async_remote_copy(
            src_ref=src,
            dst_ref=dst,
            send_sem=self.send_sem.at[k],
            recv_sem=self.recv_sem.at[k],
            device_id=self.dev(axis, step),
            device_id_type=MESH,
        )
        cp.start()
        self.sent.append(cp)
        return cp

    def barrier(self, peers):
        sem = pltpu.get_barrier_semaphore()
        for axis, step in peers:
            pl.semaphore_signal(sem, inc=1, device_id=self.dev(axis, step), device_id_type=MESH)
        pl.semaphore_wait(sem, len(peers))

    def drain(self):
        for cp in self.sent:
            cp.wait_send()


class Gather:
    def __init__(self, net, axis, piece):
        self.net, self.axis, self.piece = net, axis, piece

    def start(self):
        own = self.piece(self.net.pos(self.axis), None)
        self.up = self.net.copy(own, own, self.axis, 1)
        self.down = self.net.copy(own, own, self.axis, -1)

    def mid(self):
        self.up.wait_recv()
        low = self.piece(self.net.at(self.axis, -1), 0)
        self.up2 = self.net.copy(low, low, self.axis, 1)
        self.down.wait_recv()
        high = self.piece(self.net.at(self.axis, 1), 1)
        self.down2 = self.net.copy(high, high, self.axis, -1)

    def end(self):
        self.up2.wait_recv()
        self.down2.wait_recv()


class Scatter:
    def __init__(self, net, axis, q, bufs, add):
        self.net, self.axis, self.q, self.bufs, self.add = net, axis, q, bufs, add

    def start(self):
        lo, hi, _, _ = self.bufs
        far = self.net.at(self.axis, 2)
        self.cl = self.net.copy(self.q(far, 0), lo, self.axis, 1)
        self.ch = self.net.copy(self.q(far, 1), hi, self.axis, -1)

    def mid(self):
        lo, hi, rp, rm = self.bufs
        up, down = self.net.at(self.axis, 1), self.net.at(self.axis, -1)
        self.cl.wait_recv()
        self.add(self.q(up, 0), (lo,))
        self.cp = self.net.copy(self.q(up, None), rp, self.axis, 1)
        self.ch.wait_recv()
        self.add(self.q(down, 1), (hi,))
        self.cm = self.net.copy(self.q(down, None), rm, self.axis, -1)

    def end(self, out=None):
        _, _, rp, rm = self.bufs
        self.cp.wait_recv()
        self.cm.wait_recv()
        self.add(self.q(self.net.pos(self.axis), None), (rp, rm), out)


def add_rows(dst, srcs, out=None, out_dtype=BF):
    target = dst if out is None else out
    lead, rows = dst.shape[:-2], dst.shape[-2]
    step = 32 if rows % 32 == 0 else 16
    count = 1
    for n in lead:
        count *= n
    per = rows // step

    def body(i, _):
        r = pl.ds(pl.multiple_of(lax.rem(i, per) * step, 16), step)
        k = lax.div(i, per)
        idx = []
        for n in reversed(lead):
            idx.insert(0, lax.rem(k, n))
            k = lax.div(k, n)
        idx = (*idx, r, slice(None))
        total = dst[idx].astype(F32)
        for s in srcs:
            total += s[idx].astype(F32)
        target[idx] = total.astype(target.dtype)
        return 0

    lax.fori_loop(0, count * per, body, 0)


def weights_kernel(
    wq, wk, wv, wo, wg, wu, wd, gains, qkv_all, gu_all, wo_all, wd_all, gain_all, send_sem, recv_sem, own_sem
):
    net = Net(send_sem, recv_sem)
    y, c, x, z = net.y, net.c, net.x, net.z
    own = [
        (wq, qkv_all.at[y, :, pl.ds(0, 1024)]),
        (wk, qkv_all.at[y, :, pl.ds(1024, 256)]),
        (wv, qkv_all.at[y, :, pl.ds(1280, 256)]),
        (wo, wo_all.at[y]),
        (wg, gu_all.at[y, :, pl.ds(0, 2048)]),
        (wu, gu_all.at[y, :, pl.ds(2048, 2048)]),
        (wd, wd_all.at[y]),
        (gains, gain_all.at[y]),
    ]
    copies = []
    for k, (src, dst) in enumerate(own):
        cp = pltpu.make_async_copy(src, dst, own_sem.at[k])
        cp.start()
        copies.append(cp)
    net.barrier([("c", 1), ("x", 1), ("x", -1), ("y", 1), ("y", -1), ("y", 2), ("z", 1), ("z", -1)])
    for cp in copies:
        cp.wait()
    rows = pl.ds(pl.multiple_of(c * 80, 16), 80)

    def qkv_piece(yq, a, half):
        off, n = {None: (0, 384), 0: (0, 128), 1: (128, 256)}[half]
        return qkv_all.at[yq, rows, pl.ds(pl.multiple_of(a * 384 + off, 128), n)]

    def gu_piece(yq, a, half):
        off, n = {None: (0, 1024), 0: (0, 512), 1: (512, 512)}[half]
        return gu_all.at[yq, rows, pl.ds(pl.multiple_of(a * 1024 + off, 128), n)]

    def wo_piece(yq, a, half):
        off, n = {None: (0, 32), 0: (0, 16), 1: (16, 16)}[half]
        return wo_all.at[yq, pl.ds(pl.multiple_of(c * 128 + a * 32 + off, 16), n)]

    def wd_piece(yq, a, half):
        off, n = {None: (0, 64), 0: (0, 32), 1: (32, 32)}[half]
        return wd_all.at[yq, pl.ds(pl.multiple_of(c * 256 + a * 64 + off, 16), n)]

    def swap_of(k, yq):
        return (
            lambda: qkv_all.at[yq, rows],
            lambda: gu_all.at[yq, rows],
            lambda: wo_all.at[yq, pl.ds(pl.multiple_of(c * 128, 16), 128)],
            lambda: wd_all.at[yq, pl.ds(pl.multiple_of(c * 256, 16), 256)],
        )[k]()

    pieces = (qkv_piece, gu_piece, wo_piece, wd_piece)
    axes = ("z", "x", "z", "z")
    gain_own = gain_all.at[y]
    gain_copies = [net.copy(gain_own, gain_own, "y", s) for s in (1, -1, 2)]
    along_y = []
    for piece, axis in zip(pieces, axes):
        g = Gather(net, "y", functools.partial(lambda piece, a, yq, half: piece(yq, a, half), piece, net.pos(axis)))
        g.start()
        along_y.append(g)
    planes = {}

    def plane(k, step):
        yq = net.at("y", step)
        g = Gather(net, axes[k], functools.partial(pieces[k], yq))
        g.start()
        planes[k, step] = g

    for k in range(4):
        along_y[k].mid()
        plane(k, -1)
        plane(k, 1)
    for k in range(4):
        along_y[k].end()
        plane(k, 2)
    swaps = []
    for step in (-1, 1, 2):
        for k in range(4):
            planes[k, step].mid()
    for step in (-1, 1, 2):
        for k in range(4):
            planes[k, step].end()
            ref = swap_of(k, net.at("y", step))
            swaps.append(net.copy(ref, ref, "c"))
    for cp in (*swaps, *gain_copies):
        cp.wait_recv()
    net.drain()


def gather_weights(wq, wk, wv, wo, wg, wu, wd, gains):
    n = 3 + 16 + 48 + 12
    return pl.pallas_call(
        weights_kernel,
        out_shape=(
            jax.ShapeDtypeStruct((4, 160, 1536), BF),
            jax.ShapeDtypeStruct((4, 160, 4096), BF),
            jax.ShapeDtypeStruct((4, 256, 640), BF),
            jax.ShapeDtypeStruct((4, 512, 640), BF),
            jax.ShapeDtypeStruct((4, 16, 128), BF),
        ),
        in_specs=[ANYSPEC] * 8,
        out_specs=[ANYSPEC] * 5,
        scratch_shapes=[
            pltpu.SemaphoreType.DMA((n,)),
            pltpu.SemaphoreType.DMA((n,)),
            pltpu.SemaphoreType.DMA((8,)),
        ],
        compiler_params=pltpu.CompilerParams(collective_id=0, has_side_effects=True, vmem_limit_bytes=VMEM_LIMIT),
        name="gather_weights",
    )(wq, wk, wv, wo, wg, wu, wd, gains)


def half_rows(half):
    return {None: slice(None), 0: pl.ds(0, 64), 1: pl.ds(64, 64)}[half]


def keys_kernel(k, v, k_all, v_all, send_sem, recv_sem, own_sem):
    net = Net(send_sem, recv_sem)
    c, x, z = net.c, net.x, net.z
    own = [pltpu.make_async_copy(k, k_all.at[c, z, x], own_sem.at[0]), pltpu.make_async_copy(v, v_all.at[c, z, x], own_sem.at[1])]
    for cp in own:
        cp.start()
    net.barrier([("c", 1), ("x", 1), ("x", -1), ("z", 1), ("z", -1)])
    for cp in own:
        cp.wait()
    kx = Gather(net, "x", lambda j, h: k_all.at[c, z, j, half_rows(h)])
    vz = Gather(net, "z", lambda j, h: v_all.at[c, j, x, half_rows(h)])
    kz = Gather(net, "z", lambda j, h: k_all.at[c, j, :, half_rows(h)])
    vx = Gather(net, "x", lambda j, h: v_all.at[c, :, j, half_rows(h)])
    for g in (kx, vz):
        g.start()
    for g in (kx, vz):
        g.mid()
    for g in (kx, vz):
        g.end()
    kz.start()
    vx.start()
    swaps = []

    def swap_k(j):
        ref = k_all.at[c, j]
        swaps.append(net.copy(ref, ref, "c"))

    def swap_v(j):
        ref = v_all.at[c, :, j]
        swaps.append(net.copy(ref, ref, "c"))

    swap_k(z)
    swap_v(x)
    kz.mid()
    vx.mid()
    for s in (-1, 1):
        swap_k(net.at("z", s))
        swap_v(net.at("x", s))
    kz.end()
    vx.end()
    swap_k(net.at("z", 2))
    swap_v(net.at("x", 2))
    for cp in swaps:
        cp.wait_recv()
    net.drain()


def gather_keys(k, v):
    n = 16 + 8
    shape = jax.ShapeDtypeStruct((2, 4, 4, 128, 256), BF)
    return pl.pallas_call(
        keys_kernel,
        out_shape=(shape, shape),
        in_specs=[ANYSPEC] * 2,
        out_specs=[ANYSPEC] * 2,
        scratch_shapes=[
            pltpu.SemaphoreType.DMA((n,)),
            pltpu.SemaphoreType.DMA((n,)),
            pltpu.SemaphoreType.DMA((2,)),
        ],
        compiler_params=pltpu.CompilerParams(collective_id=1, has_side_effects=True, vmem_limit_bytes=VMEM_LIMIT),
        name="gather_keys",
    )(k, v)


def key_grads_kernel(
    dk, dv, dk_out, dv_out, kin, vin, k1lo, k1hi, k1p, k1m, v1lo, v1hi, v1p, v1m,
    k2lo, k2hi, k2p, k2m, v2lo, v2hi, v2p, v2m, send_sem, recv_sem,
):
    net = Net(send_sem, recv_sem)
    c, x, z = net.c, net.x, net.z
    net.barrier([("c", 1), ("x", 1), ("x", -1), ("z", 1), ("z", -1)])
    other = 1 - c
    kc, vc = {}, {}
    for s in (2, 1, -1, 0):
        j = net.at("z", s)
        kc[s] = net.copy(dk.at[other, j], kin.at[j], "c")
        j = net.at("x", s)
        vc[s] = net.copy(dv.at[other, :, j], vin.at[:, j], "c")

    def take(s):
        j = net.at("z", s)
        kc[s].wait_recv()
        add_rows(kin.at[j], (dk.at[c, j],))
        j = net.at("x", s)
        vc[s].wait_recv()
        add_rows(vin.at[:, j], (dv.at[c, :, j],))

    k1 = Scatter(net, "z", lambda j, h: kin.at[j, :, half_rows(h)], (k1lo, k1hi, k1p, k1m), add_rows)
    v1 = Scatter(net, "x", lambda j, h: vin.at[:, j, half_rows(h)], (v1lo, v1hi, v1p, v1m), add_rows)
    k2 = Scatter(net, "x", lambda j, h: kin.at[z, j, half_rows(h)], (k2lo, k2hi, k2p, k2m), add_rows)
    v2 = Scatter(net, "z", lambda j, h: vin.at[j, x, half_rows(h)], (v2lo, v2hi, v2p, v2m), add_rows)
    take(2)
    k1.start()
    v1.start()
    take(1)
    take(-1)
    k1.mid()
    v1.mid()
    take(0)
    k1.end()
    k2.start()
    v1.end()
    v2.start()
    k2.mid()
    v2.mid()
    k2.end(dk_out)
    v2.end(dv_out)
    net.drain()


def reduce_key_grads(dk, dv):
    n = 8 + 16
    one = jax.ShapeDtypeStruct((128, 256), F32)
    big, half_big = VMEM((4, 128, 256), BF), VMEM((4, 64, 256), BF)
    small, half_small = VMEM((128, 256), BF), VMEM((64, 256), BF)
    return pl.pallas_call(
        key_grads_kernel,
        out_shape=(one, one),
        in_specs=[VSPEC] * 2,
        out_specs=[VSPEC] * 2,
        scratch_shapes=[
            VMEM((4, 4, 128, 256), BF),
            VMEM((4, 4, 128, 256), BF),
            half_big, half_big, big, big,
            half_big, half_big, big, big,
            half_small, half_small, small, small,
            half_small, half_small, small, small,
            pltpu.SemaphoreType.DMA((n,)),
            pltpu.SemaphoreType.DMA((n,)),
        ],
        compiler_params=pltpu.CompilerParams(collective_id=2, has_side_effects=True, vmem_limit_bytes=VMEM_LIMIT),
        name="reduce_key_grads",
    )(dk, dv)


def tdot(a, b):
    return lax.dot_general(a, b, (((0,), (0,)), ((), ())), preferred_element_type=F32)


def dot(a, b):
    return jnp.dot(a, b, preferred_element_type=F32)


def dot_back(a, b):
    return lax.dot_general(a, b, (((1,), (1,)), ((), ())), preferred_element_type=F32)


PART_ORDER = (("y", "z", "x"), ("x", "y", "z"), ("z", "x", "y"))
PART_MAJOR = (("z", "x"), ("x", "z"), ("z", "x"))


def scatter_shapes(part):
    u = PART_UNITS[part]
    shapes, lead, rows = [], 4, 16 * u
    for axis in PART_ORDER[part]:
        if axis == "y":
            lead = 1
        else:
            rows //= 4
        shapes.append((lead, rows))
    return shapes


def weight_grads_kernel(*refs):
    acts, gains = refs[:8], refs[8]
    full = refs[9]
    g = refs[10]
    both = refs[11:19]
    gain_in = refs[19]
    bufs = refs[20:56]
    send_sem, recv_sem, own_sem = refs[56:]
    net = Net(send_sem, recv_sem)
    y, c, x, z = net.y, net.c, net.x, net.z
    local = []
    for k in range(8):
        cp = pltpu.make_async_copy(acts[k], both[k].at[pl.ds(0, 128)], own_sem.at[k])
        cp.start()
        local.append(cp)
    net.barrier([("c", 1), ("x", 1), ("x", -1), ("y", 1), ("y", -1), ("z", 1), ("z", -1)])
    pair = [net.copy(acts[k], both[k].at[pl.ds(128, 128)], "c") for k in range(8)]
    gain_pair = net.copy(gains, gain_in, "c")
    for k in range(8):
        local[k].wait()
        pair[k].wait_recv()
    gain_pair.wait_recv()
    normed, qkvg, attn, projg, ffn, gug, mixed, downg = both

    def put(off, n, value, col_blocks):
        value = value.astype(BF)
        for yq in range(4):
            for j in range(col_blocks):
                g[yq, pl.ds(off + j * n, n), :] = value[yq * n : yq * n + n, j * 128 : j * 128 + 128]

    def cols(start, width):
        return pl.ds(pl.multiple_of(start, 128), width)

    put(OFF_Q, 160, tdot(normed[...], qkvg[:, cols(c * 512, 512)]), 4)
    put(OFF_K, 160, tdot(normed[...], qkvg[:, cols(1024 + c * 128, 128)]), 1)
    put(OFF_V, 160, tdot(normed[...], qkvg[:, cols(1280 + c * 128, 128)]), 1)
    for part in range(2):
        put(OFF_G + part * 640, 160, tdot(ffn[...], gug[:, cols(c * 1024 + part * 512, 512)]), 4)
        put(OFF_U + part * 640, 160, tdot(ffn[...], gug[:, cols(2048 + c * 1024 + part * 512, 512)]), 4)
    for yq in range(4):
        value = tdot(attn[:, cols(yq * 256 + c * 128, 128)], projg[...]).astype(BF)
        for j in range(5):
            g[yq, pl.ds(OFF_O + j * 128, 128), :] = value[:, j * 128 : j * 128 + 128]
        value = tdot(mixed[:, cols(yq * 512 + c * 256, 256)], downg[...]).astype(BF)
        for j in range(5):
            g[yq, pl.ds(OFF_D + j * 256, 256), :] = value[:, j * 128 : j * 128 + 128]
    g[:, pl.ds(OFF_GAIN, 16), :] = (gains[...] + gain_in[...]).astype(BF)
    g[:, pl.ds(OFF_GAIN + 16, ROWS - OFF_GAIN - 16), :] = jnp.zeros((4, ROWS - OFF_GAIN - 16, 128), BF)

    place = [[0, 4, PART_OFF[p], 16 * PART_UNITS[p]] for p in range(3)]

    def share(p, axis):
        y0, yn, r0, rn = place[p]

        def q(j, half):
            if axis == "y":
                ys, yc, rs, rc = j, 1, r0, rn
            else:
                ys, yc, rs, rc = y0, yn, r0 + j * (rn // 4), rn // 4
            if half is not None:
                rc //= 2
                rs = rs + half * rc
            return g.at[pl.ds(ys, yc), pl.ds(pl.multiple_of(rs, 16), rc)]

        return q

    def narrow(p, axis):
        y0, yn, r0, rn = place[p]
        if axis == "y":
            place[p] = [y, 1, r0, rn]
        else:
            place[p] = [y0, yn, r0 + net.pos(axis) * (rn // 4), rn // 4]

    for phase in range(3):
        runs = []
        for p in range(3):
            axis = PART_ORDER[p][phase]
            k = (p * 3 + phase) * 4
            runs.append(Scatter(net, axis, share(p, axis), bufs[k : k + 4], add_rows))
            runs[-1].start()
        for r in runs:
            r.mid()
        for p, r in enumerate(runs):
            narrow(p, PART_ORDER[p][phase])
            if phase < 2:
                r.end()
            else:
                _, _, r0, rn = place[p]
                r.end(full.at[pl.ds(c, 1), pl.ds(pl.multiple_of(r0, 16), rn)])

    stages = [[], []]
    for p in range(3):
        u, off = PART_UNITS[p], PART_OFF[p]
        major, minor = PART_MAJOR[p]

        def first(j, half, u=u, off=off, major=major):
            n = u if half is None else u // 2
            return full.at[c, pl.ds(pl.multiple_of(off + net.pos(major) * 4 * u + j * u + (half or 0) * n, 16), n)]

        def second(j, half, u=u, off=off):
            n = 4 * u if half is None else 2 * u
            return full.at[c, pl.ds(pl.multiple_of(off + j * 4 * u + (half or 0) * n, 16), n)]

        stages[0].append(Gather(net, minor, first))
        stages[1].append(Gather(net, major, second))
    for r in stages[0]:
        r.start()
    for r in stages[0]:
        r.mid()
    for a, b in zip(*stages):
        a.end()
        b.start()
    for r in stages[1]:
        r.mid()
    swaps = []
    for p, r in enumerate(stages[1]):
        r.end()
        ref = full.at[c, pl.ds(PART_OFF[p], 16 * PART_UNITS[p])]
        swaps.append(net.copy(ref, ref, "c"))
    for cp in swaps:
        cp.wait_recv()
    net.drain()


def reduce_weight_grads(acts, gains):
    n = 9 + 36 + 24 + 3
    bufs = []
    for p in range(3):
        for lead, rows in scatter_shapes(p):
            bufs += [VMEM((lead, rows // 2, 128), BF)] * 2 + [VMEM((lead, rows, 128), BF)] * 2
    return pl.pallas_call(
        weight_grads_kernel,
        out_shape=jax.ShapeDtypeStruct((2, ROWS, 128), BF),
        in_specs=[VSPEC] * 9,
        out_specs=VSPEC,
        scratch_shapes=[
            VMEM((4, ROWS, 128), BF),
            *[VMEM((256, a.shape[1]), BF) for a in acts],
            VMEM((4, 16, 128), F32),
            *bufs,
            pltpu.SemaphoreType.DMA((n,)),
            pltpu.SemaphoreType.DMA((n,)),
            pltpu.SemaphoreType.DMA((8,)),
        ],
        compiler_params=pltpu.CompilerParams(collective_id=3, has_side_effects=True, vmem_limit_bytes=VMEM_LIMIT),
        name="reduce_weight_grads",
    )(*acts, gains)


def unpack_kernel(full, oq, ok, ov, oo, og, ou, od, ogain):
    for c in range(2):
        def block(off, n, j):
            return full[c, pl.ds(off + j * n, n), :].astype(F32)

        for j in range(4):
            oq[:, pl.ds(c * 512 + j * 128, 128)] = block(OFF_Q, 160, j)
        ok[:, pl.ds(c * 128, 128)] = block(OFF_K, 160, 0)
        ov[:, pl.ds(c * 128, 128)] = block(OFF_V, 160, 0)
        for j in range(8):
            og[:, pl.ds(c * 1024 + j * 128, 128)] = block(OFF_G, 160, j)
            ou[:, pl.ds(c * 1024 + j * 128, 128)] = block(OFF_U, 160, j)
        for j in range(5):
            oo[pl.ds(c * 128, 128), pl.ds(j * 128, 128)] = block(OFF_O, 128, j)
            od[pl.ds(c * 256, 256), pl.ds(j * 128, 128)] = block(OFF_D, 256, j)
    ogain[...] = full[0, pl.ds(OFF_GAIN, 16), :].astype(F32)


def unpack(full):
    def s(*shape):
        return jax.ShapeDtypeStruct(shape, F32)

    return pl.pallas_call(
        unpack_kernel,
        out_shape=(s(160, 1024), s(160, 256), s(160, 256), s(256, 640), s(160, 2048), s(160, 2048), s(512, 640), s(16, 128)),
        in_specs=[VSPEC],
        out_specs=[VSPEC] * 8,
        compiler_params=pltpu.CompilerParams(vmem_limit_bytes=VMEM_LIMIT),
        name="unpack",
    )(full)


def rms(v):
    return lax.rsqrt(jnp.mean(v * v, axis=-1, keepdims=True) + EPS)


def norm_back(v, r, g, u):
    ug = u * g
    return r * ug - v * (r * r * r) * jnp.mean(ug * v, axis=-1, keepdims=True)


def gain_grad(v, r, u):
    return jnp.sum(u * v * r, axis=0, keepdims=True)


def rope(u, cos, sin):
    a, b = u[:, :128], u[:, 128:]
    return jnp.concatenate([a * cos - b * sin, b * cos + a * sin], axis=1)


def rope_back(w, cos, sin):
    a, b = w[:, :128], w[:, 128:]
    return jnp.concatenate([a * cos + b * sin, b * cos - a * sin], axis=1)


def project_kernel(tokens, g_in, w, g_q, g_k, cos, sin, q, k, v, normed_out, raw):
    t = tokens[...].astype(F32)
    normed = (t * rms(t) * g_in[...]).astype(BF)
    normed_out[...] = normed
    weights = w[...].reshape(640, 1536)
    both = dot(normed, weights)
    raw[...] = both[:, :1280]
    for h in range(4):
        u = both[:, h * 256 : h * 256 + 256]
        q[pl.ds(h * 128, 128), :] = (rope(u * rms(u) * g_q[...], cos[...], sin[...]).astype(BF) * 0.0625).astype(BF)
    u = both[:, 1024:1280]
    k[...] = rope(u * rms(u) * g_k[...], cos[...], sin[...]).astype(BF)
    v[...] = both[:, 1280:1536].astype(BF)


def project(tokens, g_in, w, g_q, g_k, cos, sin):
    def s(dtype, *shape):
        return jax.ShapeDtypeStruct(shape, dtype)

    return pl.pallas_call(
        project_kernel,
        out_shape=(s(BF, 512, 256), s(BF, 128, 256), s(BF, 128, 256), s(BF, 128, 640), s(F32, 128, 1280)),
        in_specs=[VSPEC] * 7,
        out_specs=[VSPEC] * 5,
        compiler_params=pltpu.CompilerParams(vmem_limit_bytes=VMEM_LIMIT),
        name="project",
    )(tokens, g_in, w, g_q, g_k, cos, sin)


def causal(x, c_key):
    me = lax.axis_index("ctx")
    start = lax.rem(me, 8) * 128
    row = lax.broadcasted_iota(jnp.int32, (512, 512), 0)
    col = lax.broadcasted_iota(jnp.int32, (512, 512), 1)
    q_pos = start + (row & 127)
    k_pos = (col >> 7) * 256 + c_key * 128 + (col & 127)
    return k_pos <= q_pos


def main_kernel(
    q, k_all, v_all, tokens, cot, w_gu, w_o, w_d, g_post, g_pre, g_fpost,
    layer_out, hidden_grad_out, dq_out, dk, dv, attn_out, projg_out, ffn_out, gug_out, mixed_out, downg_out,
    gg_post, gg_pre, gg_fpost,
    acc, row_sum, gate_s, up_s,
):
    z = lax.div(lax.axis_index("ctx"), 8)
    queries = q[...]
    acc[...] = jnp.zeros_like(acc)
    row_sum[...] = jnp.zeros_like(row_sum)

    def keys_of(c, j):
        return k_all[c, j].reshape(512, 256), v_all[c, j].reshape(512, 256)

    def fwd(c, j, diagonal):
        kt, vt = keys_of(c, j)
        p = jnp.exp(dot_back(queries, kt))
        if diagonal:
            p = jnp.where(causal(None, c), p, 0.0)
        row_sum[...] += jnp.sum(p, axis=1, keepdims=True)
        acc[...] += dot(p.astype(BF), vt)

    def fwd_step(i, _):
        fwd(lax.rem(i, 2), lax.div(i, 2), False)
        return 0

    lax.fori_loop(0, z * 2, fwd_step, 0)
    fwd(0, z, True)
    fwd(1, z, True)
    inv = 1.0 / row_sum[...]
    row_sum[...] = inv
    attended = acc[...] * inv
    acc[...] = attended
    attn = jnp.concatenate([attended[h * 128 : h * 128 + 128] for h in range(4)], axis=1).astype(BF)
    attn_out[...] = attn
    wo = w_o[...].reshape(1024, 640)
    wd = w_d[...].reshape(2048, 640)
    gu = w_gu.reshape(640, 4096)
    proj = dot(attn, wo)
    r_proj = rms(proj)
    hidden = tokens[...].astype(F32) + proj * r_proj * g_post[...]
    r_hidden = rms(hidden)
    ffn = (hidden * r_hidden * g_pre[...]).astype(BF)
    ffn_out[...] = ffn
    for i in range(4):
        cs = pl.ds(i * 512, 512)
        gate = dot(ffn, gu[:, cs])
        up = dot(ffn, gu[:, pl.ds(2048 + i * 512, 512)])
        t = jnp.tanh(C_ROOT * (gate + C_CUBE * gate * gate * gate))
        gelu = 0.5 * gate * (1.0 + t)
        slope = 0.5 * (1.0 + t) + 0.5 * gate * (1.0 - t * t) * (C_ROOT * (1.0 + 3.0 * C_CUBE * gate * gate))
        mixed_out[:, cs] = (gelu * up).astype(BF)
        gate_s[:, cs] = up * slope
        up_s[:, cs] = gelu
    down = dot(mixed_out[...], wd)
    r_down = rms(down)
    layer_out[...] = (hidden + down * r_down * g_fpost[...]).astype(BF)
    out_grad = cot[...].astype(F32)
    down_grad = norm_back(down, r_down, g_fpost[...], out_grad).astype(BF)
    gg_fpost[...] = gain_grad(down, r_down, out_grad)
    downg_out[...] = down_grad
    for i in range(4):
        cs = pl.ds(i * 512, 512)
        mg = dot_back(down_grad, wd[i * 512 : i * 512 + 512])
        gug_out[:, cs] = (mg * gate_s[:, cs]).astype(BF)
        gug_out[:, pl.ds(2048 + i * 512, 512)] = (mg * up_s[:, cs]).astype(BF)
    ffn_grad = dot_back(gug_out[...], gu[...])
    hidden_grad = out_grad + norm_back(hidden, r_hidden, g_pre[...], ffn_grad)
    gg_pre[...] = gain_grad(hidden, r_hidden, ffn_grad)
    hidden_grad_out[...] = hidden_grad
    proj_grad = norm_back(proj, r_proj, g_post[...], hidden_grad).astype(BF)
    gg_post[...] = gain_grad(proj, r_proj, hidden_grad)
    projg_out[...] = proj_grad
    attn_grad = dot_back(proj_grad, wo).astype(BF)
    do = jnp.concatenate([attn_grad[:, h * 256 : h * 256 + 256] for h in range(4)], axis=0)
    delta = jnp.sum(do.astype(F32) * acc[...], axis=1, keepdims=True)
    acc[...] = jnp.zeros_like(acc)

    def bwd(c, j, diagonal):
        kt, vt = keys_of(c, j)
        p = jnp.exp(dot_back(queries, kt)) * row_sum[...]
        if diagonal:
            p = jnp.where(causal(None, c), p, 0.0)
        ds = (p * (dot_back(do, vt) - delta)).astype(BF)
        acc[...] += dot(ds, kt)
        dk[c, j] = tdot(ds, queries).astype(BF).reshape(4, 128, 256)
        dv[c, j] = tdot(p.astype(BF), do).astype(BF).reshape(4, 128, 256)

    def bwd_step(i, _):
        bwd(lax.rem(i, 2), lax.div(i, 2), False)
        return 0

    def zero_step(i, _):
        zero = jnp.zeros((4, 128, 256), BF)
        dk[lax.rem(i, 2), lax.div(i, 2)] = zero
        dv[lax.rem(i, 2), lax.div(i, 2)] = zero
        return 0

    lax.fori_loop(0, z * 2, bwd_step, 0)
    bwd(0, z, True)
    bwd(1, z, True)
    lax.fori_loop(z * 2 + 2, 8, zero_step, 0)
    dq_out[...] = acc[...] * 0.0625


def main_part(q, k_all, v_all, tokens, cot, w_gu, w_o, w_d, g_post, g_pre, g_fpost):
    def s(dtype, *shape):
        return jax.ShapeDtypeStruct(shape, dtype)

    return pl.pallas_call(
        main_kernel,
        out_shape=(
            s(BF, 128, 640), s(F32, 128, 640), s(F32, 512, 256), s(BF, 2, 4, 4, 128, 256), s(BF, 2, 4, 4, 128, 256),
            s(BF, 128, 1024), s(BF, 128, 640), s(BF, 128, 640), s(BF, 128, 4096), s(BF, 128, 2048), s(BF, 128, 640),
            s(F32, 1, 640), s(F32, 1, 640), s(F32, 1, 640),
        ),
        in_specs=[VSPEC] * 11,
        out_specs=[VSPEC] * 14,
        scratch_shapes=[VMEM((512, 256), F32), VMEM((512, 1), F32), VMEM((128, 2048), F32), VMEM((128, 2048), F32)],
        compiler_params=pltpu.CompilerParams(vmem_limit_bytes=VMEM_LIMIT),
        name="main_part",
    )(q, k_all, v_all, tokens, cot, w_gu, w_o, w_d, g_post, g_pre, g_fpost)


def finish_kernel(
    dq, dk, dv, raw, cos, sin, g_q, g_k, w, tokens, g_in, hidden_grad,
    input_grad, qkvg, gg_q, gg_k, gg_in,
):
    total_q = jnp.zeros((1, 256), F32)
    for h in range(4):
        v = raw[:, pl.ds(h * 256, 256)]
        r = rms(v)
        u = rope_back(dq[pl.ds(h * 128, 128), :], cos[...], sin[...])
        total_q += gain_grad(v, r, u)
        qkvg[:, pl.ds(h * 256, 256)] = norm_back(v, r, g_q[...], u).astype(BF)
    gg_q[...] = total_q
    v = raw[:, pl.ds(1024, 256)]
    r = rms(v)
    u = rope_back(dk[...], cos[...], sin[...])
    gg_k[...] = gain_grad(v, r, u)
    qkvg[:, pl.ds(1024, 256)] = norm_back(v, r, g_k[...], u).astype(BF)
    qkvg[:, pl.ds(1280, 256)] = dv[...].astype(BF)
    normed_grad = dot_back(qkvg[...], w[...].reshape(640, 1536))
    t = tokens[...].astype(F32)
    r = rms(t)
    gg_in[...] = gain_grad(t, r, normed_grad)
    input_grad[...] = hidden_grad[...] + norm_back(t, r, g_in[...], normed_grad)


def finish(*args):
    def s(dtype, *shape):
        return jax.ShapeDtypeStruct(shape, dtype)

    return pl.pallas_call(
        finish_kernel,
        out_shape=(s(F32, 128, 640), s(BF, 128, 1536), s(F32, 1, 256), s(F32, 1, 256), s(F32, 1, 640)),
        in_specs=[VSPEC] * 12,
        out_specs=[VSPEC] * 5,
        compiler_params=pltpu.CompilerParams(vmem_limit_bytes=VMEM_LIMIT),
        name="finish",
    )(*args)


GAIN_SIZES = (160, 64, 64, 160, 160, 160)


def local(
    tokens, positions, w_query, w_key, w_value, w_out, w_gate, w_up, w_down,
    gain_in, gain_query, gain_key, gain_attn_post, gain_ffn_pre, gain_ffn_post, cotangent,
):
    gains = jnp.concatenate(
        [gain_in, gain_query, gain_key, gain_attn_post, gain_ffn_pre, gain_ffn_post, jnp.zeros((1280,), BF)]
    ).reshape(16, 128)
    w_qkv, w_gu, w_o, w_d, gain_all = gather_weights(w_query, w_key, w_value, w_out, w_gate, w_up, w_down, gains)
    flat = gain_all.reshape(4, 2048).astype(F32)
    parts, start = [], 0
    for n in GAIN_SIZES:
        parts.append(flat[:, start : start + n].reshape(1, 4 * n))
        start += n
    g_in, g_q, g_k, g_post, g_pre, g_fpost = parts
    exponents = jnp.arange(0, 256, 2, dtype=F32) / 256
    inverse = 1.0 / ROPE_BASE**exponents
    angles = positions.astype(F32)[:, None] * inverse[None, :]
    cos, sin = jnp.cos(angles), jnp.sin(angles)
    q, k, v, normed, raw = project(tokens, g_in, w_qkv, g_q, g_k, cos, sin)
    k_all, v_all = gather_keys(k, v)
    (
        layer_out, hidden_grad, dq, dk, dv, attn, projg, ffn, gug, mixed, downg, gg_post, gg_pre, gg_fpost,
    ) = main_part(q, k_all, v_all, tokens, cotangent, w_gu, w_o, w_d, g_post, g_pre, g_fpost)
    dk_own, dv_own = reduce_key_grads(dk, dv)
    input_grad, qkvg, gg_q, gg_k, gg_in = finish(
        dq, dk_own, dv_own, raw, cos, sin, g_q, g_k, w_qkv, tokens, g_in, hidden_grad
    )
    gain_grads = jnp.concatenate(
        [a.reshape(4, n) for a, n in zip((gg_in, gg_q, gg_k, gg_post, gg_pre, gg_fpost), GAIN_SIZES)]
        + [jnp.zeros((4, 1280), F32)],
        axis=1,
    ).reshape(4, 16, 128)
    full = reduce_weight_grads((normed, qkvg, attn, projg, ffn, gug, mixed, downg), gain_grads)
    oq, ok, ov, oo, og, ou, od, ogain = unpack(full)
    flat = ogain.reshape(2048)
    outs, start = [], 0
    for n in GAIN_SIZES:
        outs.append(flat[start : start + n])
        start += n
    return (layer_out, input_grad, oq, ok, ov, oo, og, ou, od, *outs)


def solution(mesh):
    rows, both, vec = P("fsdp", None), P(("fsdp", "ctx"), None), P("fsdp")
    in_specs = (both, P(("fsdp", "ctx")), *[rows] * 7, *[vec] * 6, both)
    out_specs = (both, both, *[rows] * 7, *[vec] * 6)
    return jax.shard_map(local, mesh=mesh, in_specs=in_specs, out_specs=out_specs, check_vma=False)
```

time: 656 us -> 311 us (0.47)
  waiting for transfers between devices: 444 us -> 0 us
  Pallas kernels: 0 us -> 291 us
  blocking collectives: 81.4 us -> 0 us
  matrix products: 42.2 us -> 0 us
  other arithmetic: 37.5 us -> 5.09 us
  between operations: 17.6 us -> 0.76 us
  local copies, waits for them, and re-layouts: 29 us -> 13.4 us
    pallas_call x0 -> x8, Pallas kernels: none -> 291 us  [the longest x1 122 us: gather_weights(): pl.pallas_call(weights_kernel, out_shape=(jax.ShapeDtypeStruct((4, 160, 1...]
    reduce_scatter x5 -> x0, waiting for transfers between devices: 253 us -> none  [the longest x3 192 us: sent_together(): whole = lax.psum_scatter(both, axis, scatter_dimension=dim, tiled=True)]
    all_gather x5 -> x0, waiting for transfers between devices: 156 us -> none  [the longest x3 113 us: side_by_side(): whole = lax.all_gather(both, axis, axis=dim, tiled=True)]
    psum x1 -> x0, blocking collectives: 64.9 us -> none  [local(): lax.psum(attn_shares[4].astype(jnp.bfloat16), 'ctx').astype(jnp.float32)]
    dot_general x28 -> x0, matrix products: 42.2 us -> none  [the longest x10 13.6 us: dot_back(): lax.dot_general(left_side, right_side, (((1,), (1,)), ((), ())), preferre...]
    psum x1 -> x0, waiting for transfers between devices: 33.5 us -> none  [local(): lax.psum(attn_shares[0].astype(jnp.bfloat16), 'ctx').astype(jnp.float32)]
    convert_element_type x27 -> x1, other arithmetic: 18.3 us -> 0.01 us  [local(): angles = positions.astype(F32)[:, None] * inverse[None, :]]
    unnamed x2 -> x0, blocking collectives: 16.5 us -> none
  transfers between devices with their start and end apart: 11 -> 0, of which waited for: 11 -> 0; matrix products, arithmetic and copies ran while one was open for 9% -> 0% of each run, Pallas kernels for 0% -> 0%
where the time goes in v1:
time: 311 us
  Pallas kernels  291 us (94%)
  local copies, waits for them, and re-layouts  13.4 us (4%)
  other arithmetic  5.09 us (2%)
    pallas_call x1, Pallas kernels, gather_weights(): pl.pallas_call(weights_kernel, out_shape=(jax.ShapeDtypeStruct((4, 160, 1...  122 us
    pallas_call x1, Pallas kernels, reduce_weight_grads(): pl.pallas_call(weight_grads_kernel, out_shape=jax.ShapeDtypeStruct((2, RO...  74.8 us
    pallas_call x1, Pallas kernels, reduce_key_grads(): pl.pallas_call(key_grads_kernel, out_shape=(one, one), in_specs=[VSPEC] *...  36.1 us
    pallas_call x1, Pallas kernels, gather_keys(): pl.pallas_call(keys_kernel, out_shape=(shape, shape), in_specs=[ANYSPEC]...  29.5 us
    pallas_call x1, Pallas kernels, main_part(): pl.pallas_call(main_kernel, out_shape=(s(BF, 128, 640), s(F32, 128, 640),...  17.5 us

profile of v1, /device:TPU:1, one launch (start us, length us, event | category | flops | bytes accessed | tf_op | source)
XLA Modules:
  0.0 310.6 jit_solution(13939316614570244429)
XLA Ops:
  0.7 4.7 %concatenate.6 = bf16[2048]{0:T(1024)(128)(2,1)} concatenate(bf16[160]{0:T(256)(128)(2,1)} %param.25, bf16[64]{0:T(256)(128)(2,1)} %param.26, bf16[64]{0:T(256)(128)(2,1)} %param.27, bf16[160]{0:T(256)(128)(2,1)} %param.28, bf16[160]{0:T(256)(128)(2,1)} %param.29, bf16[160]{0:T(256)(128)(2,1)} %param.30, bf16[1280]{0:T(1024)(128)(2,1)S(1)} %broadcast_in_dim.8), dimensions={0} | concatenate | bytes 8192 | tf_op jit(solution)/shard_map/concatenate | solution.py:850
  5.4 122.0 %gather_weights.1 = (bf16[4,160,1536]{2,1,0:T(8,128)(2,1)}, bf16[4,160,4096]{2,1,0:T(8,128)(2,1)}, bf16[4,256,640]{2,1,0:T(8,128)(2,1)}, bf16[4,512,640]{2,1,0:T(8,128)(2,1)}, bf16[4,16,128]{2,1,0:T(8,128)(2,1)}) custom-call(bf16[160,1024]{1,0:T(8,128)(2,1)} %wq.1, bf16[160,256]{1,0:T(8,128)(2,1)} %wk.1, bf16[160,256]{1,0:T(8,128)(2,1)} %wv.1, ...), custom_call_target="tpu_custom_call" | custom-call | tf_op jit(solution)/shard_map/gather_weights/pallas_call | solution.py:248
  127.4 0.7 convert_bitcast_fusion
  128.1 0.1 fusion
  128.2 0.7 reshape.86.g_in
  128.9 0.6 reshape.87.g_q
  129.6 0.6 reshape.88.g_k
  130.2 1.0 multiply_sine_fusion
  131.2 3.3 %project.1 = (bf16[512,256]{1,0:T(8,128)(2,1)}, bf16[128,256]{1,0:T(8,128)(2,1)}, bf16[128,256]{1,0:T(8,128)(2,1)}, bf16[128,640]{1,0:T(8,128)(2,1)}, f32[128,1280]{1,0:T(8,128)}) custom-call(bf16[128,640]{1,0:T(8,128)(2,1)} %tokens.5, f32[1,640]{1,0:T(1,128)} %reshape.86.g_in, bf16[4,160,1536]{2,1,0:T(8,128)(2,1)} %get-tuple-element.57.w, ...), custom_call_target="tpu_custom_call" | custom-call | tf_op jit(solution)/shard_map/project/pallas_call | solution.py:660
  134.4 29.5 %gather_keys.1 = (bf16[2,4,4,128,256]{4,3,2,1,0:T(8,128)(2,1)}, bf16[2,4,4,128,256]{4,3,2,1,0:T(8,128)(2,1)}) custom-call(bf16[128,256]{1,0:T(8,128)(2,1)} %get-tuple-element.59.k, bf16[128,256]{1,0:T(8,128)(2,1)} %get-tuple-element.60.v), custom_call_target="tpu_custom_call" | custom-call | tf_op jit(solution)/shard_map/gather_keys/pallas_call | solution.py:323
  163.9 0.7 reshape.89.g_post
  164.6 0.7 reshape.90.g_pre
  165.2 0.7 reshape.91.g_fpost
  165.9 17.5 %main_part.1 = (bf16[128,640]{1,0:T(8,128)(2,1)}, f32[128,640]{1,0:T(8,128)}, f32[512,256]{1,0:T(8,128)}, bf16[2,4,4,128,256]{4,3,2,1,0:T(8,128)(2,1)}, bf16[2,4...) custom-call(bf16[512,256]{1,0:T(8,128)(2,1)} %get-tuple-element.58.q, ...), custom_call_target="tpu_custom_call" | custom-call | tf_op jit(solution)/shard_map/main_part/pallas_call | solution.py:789
  183.5 36.1 %reduce_key_grads.1 = (f32[128,256]{1,0:T(8,128)}, f32[128,256]{1,0:T(8,128)}) custom-call(bf16[2,4,4,128,256]{4,3,2,1,0:T(8,128)(2,1)} %get-tuple-element.68.dk, bf16[2,4,4,128,256]{4,3,2,1,0:T(8,128)(2,1)} %get-tuple-element.69.dv), custom_call_target="tpu_custom_call" | custom-call | tf_op jit(solution)/shard_map/reduce_key_grads/pallas_call | solution.py:389
  219.6 3.8 %finish.1 = (f32[128,640]{1,0:T(8,128)}, bf16[128,1536]{1,0:T(8,128)(2,1)}, f32[1,256]{1,0:T(1,128)}, f32[1,256]{1,0:T(1,128)}, f32[1,640]{1,0:T(1,128)}) custom-call(f32[512,256]{1,0:T(8,128)} %get-tuple-element.67.dq, f32[128,256]{1,0:T(8,128)} %get-tuple-element.70.dk, f32[128,256]{1,0:T(8,128)} %get-tuple-element.71.dv, ...), custom_call_target="tpu_custom_call" | custom-call | tf_op jit(solution)/shard_map/finish/pallas_call | solution.py:833
  223.4 0.7 reduce
  224.0 0.1 reshape.92
  224.1 0.5 broadcast.23
  224.6 1.3 reduce.10
  226.0 0.1 reshape.93
  226.1 1.3 reduce.11
  227.4 0.1 reshape.94
  227.5 0.1 reshape.95
  227.6 0.1 reshape.96
  227.7 0.1 reshape.97
  227.8 0.1 concatenate.7
  227.9 0.6 copy.35
  228.5 74.8 %reduce_weight_grads.1.full = bf16[2,5632,128]{2,1,0:T(8,128)(2,1)} custom-call(bf16[128,640]{1,0:T(8,128)(2,1)} %get-tuple-element.75.refs_0_, bf16[128,1536]{1,0:T(8,128)(2,1)} %get-tuple-element.76.refs_1_, bf16[128,1024]{1,0:T(8,128)(2,1)} %get-tuple-element.77.refs_2_, bf16[128,640]{1,0:T(8,128)(2,1)} %get-tuple-element.78.refs_3_, ...), custom_call_target="tpu_custom_call" | custom-call | tf_op jit(solution)/shard_map/reduce_weight_grads/pallas_call | solution.py:567
  303.4 4.4 %unpack.1 = (f32[160,1024]{1,0:T(8,128)}, f32[160,256]{1,0:T(8,128)}, f32[160,256]{1,0:T(8,128)}, f32[256,640]{1,0:T(8,128)}, f32[160,2048]{1,0:T(8,128)}, /*ind...) custom-call(bf16[2,5632,128]{2,1,0:T(8,128)(2,1)} %reduce_weight_grads.1.full), custom_call_target="tpu_custom_call" | custom-call | tf_op jit(solution)/shard_map/unpack/pallas_call | solution.py:608
  307.8 1.5 fusion.2
  309.2 1.3 fusion.3
  (17 shorter events, 0.2 us)
Async XLA Ops:
  0.6 129.6 %copy-start.3 = (s32[128]{0:T(128)S(1)}, s32[128]{0:T(128)}, u32[]{:S(2)}) copy-start(s32[128]{0:T(128)} %param.17) | copy-start | bytes 1540
  219.5 8.0 %copy-start.2 = (f32[1,640]{1,0:T(1,128)S(1)}, f32[1,640]{1,0:T(1,128)}, u32[]{:S(2)}) copy-start(f32[1,640]{1,0:T(1,128)} %get-tuple-element.86) | copy-start | bytes 7684
  219.5 8.0 %copy-start.1 = (f32[1,640]{1,0:T(1,128)S(1)}, f32[1,640]{1,0:T(1,128)}, u32[]{:S(2)}) copy-start(f32[1,640]{1,0:T(1,128)} %get-tuple-element.87) | copy-start | bytes 7684
  219.5 8.1 %copy-start = (f32[1,640]{1,0:T(1,128)S(1)}, f32[1,640]{1,0:T(1,128)}, u32[]{:S(2)}) copy-start(f32[1,640]{1,0:T(1,128)} %get-tuple-element.88) | copy-start | bytes 7684

commit v2 on v0

v2 whole, which is shorter than its diff:
```python
import functools

import jax
import jax.numpy as jnp
from jax import lax
from jax.experimental import pallas as pl
from jax.experimental.pallas import tpu as pltpu
from jax.sharding import PartitionSpec as P

EPS = 1e-06
ROPE_BASE = 1000000.0
BF = jnp.bfloat16
F32 = jnp.float32
MESH = pl.DeviceIdType.MESH
VMEM = pltpu.VMEM
VSPEC = pl.BlockSpec(memory_space=pltpu.VMEM)
ANYSPEC = pl.BlockSpec(memory_space=pl.ANY)
VMEM_LIMIT = 60 * 1024 * 1024
C_ROOT = 0.7978845608028654
C_CUBE = 0.044715

E_ROWS, M_ROWS, L_ROWS = 4608, 768, 512
OFF_G, OFF_U, OFF_O, OFF_D, E_END = 0, 1280, 2560, 3200, 4480
OFF_Q, M_END = 0, 640
OFF_K, OFF_V, OFF_GAIN, L_END = 0, 160, 320, 336
EA_PARTS = ((0, 2560, "yzx"),)
EB_PARTS = ((2560, 1024, "xzy"), (3584, 1024, "zxy"))
M_PARTS = ((0, 256, "yzx"), (256, 256, "xzy"), (512, 256, "zxy"))
L_PARTS = ((0, 256, "yzx"), (256, 256, "xyz"))
GAIN_SIZES = (160, 64, 64, 160, 160, 160)
STEPS = (2, 1, -1)


class Net:
    def __init__(self, send_sem, recv_sem):
        me = lax.axis_index("ctx")
        self.y = lax.axis_index("fsdp")
        self.c = lax.rem(me, 2)
        self.x = lax.rem(lax.div(me, 2), 4)
        self.z = lax.div(me, 8)
        self.send_sem, self.recv_sem = send_sem, recv_sem
        self.used = 0
        self.sent = []

    def pos(self, axis):
        return {"x": self.x, "y": self.y, "z": self.z}[axis]

    def at(self, axis, step):
        return lax.rem(self.pos(axis) + (step + 4), 4)

    def dev(self, axis, step):
        x, y, z, c = self.x, self.y, self.z, self.c
        if axis == "x":
            x = self.at("x", step)
        elif axis == "y":
            y = self.at("y", step)
        elif axis == "z":
            z = self.at("z", step)
        else:
            c = 1 - c
        return {"fsdp": y, "ctx": z * 8 + x * 2 + c}

    def copy(self, src, dst, axis, step=1):
        k = self.used
        self.used += 1
        cp = pltpu.make_async_remote_copy(
            src_ref=src,
            dst_ref=dst,
            send_sem=self.send_sem.at[k],
            recv_sem=self.recv_sem.at[k],
            device_id=self.dev(axis, step),
            device_id_type=MESH,
        )
        cp.start()
        self.sent.append(cp)
        return cp

    def barrier(self):
        sem = pltpu.get_barrier_semaphore()
        peers = [("c", 1), *[(a, s) for a in "xyz" for s in STEPS]]
        for axis, step in peers:
            pl.semaphore_signal(sem, inc=1, device_id=self.dev(axis, step), device_id_type=MESH)
        pl.semaphore_wait(sem, len(peers))

    def drain(self):
        for cp in self.sent:
            cp.wait_send()


class Relay:
    def __init__(self, net, axis, piece, own):
        self.net, self.axis, self.piece, self.own = net, axis, piece, own

    def start(self):
        self.up = [self.net.copy(a, b, self.axis, 1) for a, b in self.own]
        self.down = [self.net.copy(a, b, self.axis, -1) for a, b in self.own]

    def mid(self):
        for cp in self.up:
            cp.wait_recv()
        low = self.piece(self.net.at(self.axis, -1), 0)
        self.up2 = self.net.copy(low, low, self.axis, 1)
        for cp in self.down:
            cp.wait_recv()
        high = self.piece(self.net.at(self.axis, 1), 1)
        self.down2 = self.net.copy(high, high, self.axis, -1)

    def end(self):
        self.up2.wait_recv()
        self.down2.wait_recv()


class Gather:
    def __init__(self, net, axis, piece):
        self.net, self.axis, self.piece = net, axis, piece

    def start(self):
        own = self.piece(self.net.pos(self.axis))
        self.copies = [(s, self.net.copy(own, own, self.axis, s)) for s in (1, -1, 2)]

    def end(self, then=None):
        for s, cp in self.copies:
            cp.wait_recv()
            if then is not None:
                then(self.net.at(self.axis, -s))


class Scatter:
    def __init__(self, net, axis, q, bufs):
        self.net, self.axis, self.q, self.bufs = net, axis, q, bufs
        self.copies = []

    def send(self, s):
        buf = self.bufs[STEPS.index(s)]
        self.copies.append(self.net.copy(self.q(self.net.at(self.axis, s)), buf, self.axis, s))

    def start(self):
        for s in STEPS:
            self.send(s)

    def end(self, out=None):
        for cp in self.copies:
            cp.wait_recv()
        add_rows(self.q(self.net.pos(self.axis)), self.bufs, out)


def add_rows(dst, srcs, out=None):
    target = dst if out is None else out
    lead, rows = dst.shape[:-2], dst.shape[-2]
    step = next(n for n in (256, 192, 128, 96, 64, 48, 32, 16) if rows % n == 0)
    per = rows // step
    count = per
    for n in lead:
        count *= n

    def body(i, _):
        idx = []
        k = lax.div(i, per)
        for n in reversed(lead):
            idx.insert(0, lax.rem(k, n))
            k = lax.div(k, n)
        idx = (*idx, pl.ds(pl.multiple_of(lax.rem(i, per) * step, 16), step), slice(None))
        total = dst[idx].astype(F32)
        for s in srcs:
            total += s[idx].astype(F32)
        target[idx] = total.astype(target.dtype)
        return 0

    lax.fori_loop(0, count, body, 0)


def tdot(a, b):
    return lax.dot_general(a, b, (((0,), (0,)), ((), ())), preferred_element_type=F32)


def dot(a, b):
    return jnp.dot(a, b, preferred_element_type=F32)


def dot_back(a, b):
    return lax.dot_general(a, b, (((1,), (1,)), ((), ())), preferred_element_type=F32)


def rms(v):
    return lax.rsqrt(jnp.mean(v * v, axis=-1, keepdims=True) + EPS)


def norm_back(v, r, g, u):
    ug = u * g
    return r * ug - v * (r * r * r) * jnp.mean(ug * v, axis=-1, keepdims=True)


def gain_grad(v, r, u):
    return jnp.sum(u * v * r, axis=0, keepdims=True)


def rope(u, cos, sin):
    a, b = u[:, :128], u[:, 128:]
    return jnp.concatenate([a * cos - b * sin, b * cos + a * sin], axis=1)


def rope_back(w, cos, sin):
    a, b = w[:, :128], w[:, 128:]
    return jnp.concatenate([a * cos + b * sin, b * cos - a * sin], axis=1)


def causal(net, c_key):
    row = lax.broadcasted_iota(jnp.int32, (512, 512), 0)
    col = lax.broadcasted_iota(jnp.int32, (512, 512), 1)
    q_pos = (net.x * 2 + net.c) * 128 + (row & 127)
    k_pos = (col >> 7) * 256 + c_key * 128 + (col & 127)
    return k_pos <= q_pos


class Group:
    def __init__(self, net, g, full, parts, bufs):
        self.net, self.g, self.full, self.parts, self.bufs = net, g, full, parts, bufs
        self.place = [[0, 4, off, rows] for off, rows, _ in parts]
        self.phase = -1

    def q(self, p, axis):
        y0, yn, r0, rn = self.place[p]

        def share(j):
            if axis == "y":
                return self.g.at[pl.ds(j, 1), pl.ds(pl.multiple_of(r0, 16), rn)]
            return self.g.at[pl.ds(y0, yn), pl.ds(pl.multiple_of(r0 + j * (rn // 4), 16), rn // 4)]

        return share

    def scatter_start(self, phase):
        self.runs = []
        for p, (_, _, order) in enumerate(self.parts):
            k = (p * 3 + phase) * 3
            self.runs.append(Scatter(self.net, order[phase], self.q(p, order[phase]), self.bufs[k : k + 3]))
            self.runs[-1].start()

    def scatter_end(self, phase):
        for p, r in enumerate(self.runs):
            y0, yn, r0, rn = self.place[p]
            axis = self.parts[p][2][phase]
            if axis == "y":
                self.place[p] = [self.net.y, 1, r0, rn]
            else:
                self.place[p] = [y0, yn, r0 + self.net.pos(axis) * (rn // 4), rn // 4]
            _, _, r0, rn = self.place[p]
            r.end(self.full.at[pl.ds(self.net.c, 1), pl.ds(pl.multiple_of(r0, 16), rn)] if phase == 2 else None)

    def gather_start(self, stage):
        self.runs = []
        for off, rows, order in self.parts:
            u = rows // 16
            major, minor = order.replace("y", "")

            def piece(j, u=u, off=off, major=major):
                if stage == 0:
                    return self.full.at[self.net.c, pl.ds(pl.multiple_of(off + self.net.pos(major) * 4 * u + j * u, 16), u)]
                return self.full.at[self.net.c, pl.ds(pl.multiple_of(off + j * 4 * u, 16), 4 * u)]

            self.runs.append(Gather(self.net, minor if stage == 0 else major, piece))
            self.runs[-1].start()

    def step(self):
        done, self.phase = self.phase, self.phase + 1
        if 0 <= done < 3:
            self.scatter_end(done)
        elif 3 <= done < 5:
            for r in self.runs:
                r.end()
        elif done == 5:
            self.swap.wait_recv()
        if done < 2:
            self.scatter_start(done + 1)
        elif done < 4:
            self.gather_start(done - 2)
        elif done == 4:
            ref = self.full.at[self.net.c, pl.ds(self.parts[0][0], sum(rows for _, rows, _ in self.parts))]
            self.swap = self.net.copy(ref, ref, "c")


def group_bufs(parts):
    bufs = []
    for _, rows, order in parts:
        lead = 4
        for axis in order:
            if axis == "y":
                lead = 1
            else:
                rows //= 4
            bufs += [VMEM((lead, rows, 128), BF)] * 3
    return bufs


ALL_PARTS = (EA_PARTS, EB_PARTS, M_PARTS, L_PARTS)


def layer_kernel(*refs):
    refs = list(refs)

    def take_refs(n):
        out = refs[:n]
        del refs[:n]
        return out

    wq, wk, wv, wo, wg, wu, wd = take_refs(7)
    gain_ins = take_refs(6)
    tokens, cot, cos, sin = take_refs(4)
    layer_out, input_grad, e_full, m_full, l_full = take_refs(5)
    qkv_all, gu, wo_all, wd_all, k_all, v_all = take_refs(6)
    normed, qkvg, attn, projg, ffn, gug, mixed, downg = take_refs(8)
    gain_all, gains, gain_s, gain_other, ge, gm, gl = take_refs(7)
    dk, dv, kin, vin, acc, inv_s, delta_s, do_s, q_s, raw, f_s, g_s, hidden_grad_s = take_refs(13)
    kbufs, vbufs, k2bufs, v2bufs = take_refs(3), take_refs(3), take_refs(3), take_refs(3)
    group_b = [take_refs(9 * len(parts)) for parts in ALL_PARTS]
    send_sem, recv_sem, own_sem = take_refs(3)
    net = Net(send_sem, recv_sem)
    y, c, x, z = net.y, net.c, net.x, net.z
    other = 1 - c
    own_rows, other_rows = pl.ds(0, 128), pl.ds(128, 128)
    own = []
    for k, (src, dst) in enumerate(
        [
            (wg, gu.at[y, :, pl.ds(0, 2048)]), (wu, gu.at[y, :, pl.ds(2048, 2048)]),
            (wq, qkv_all.at[y, :, pl.ds(0, 1024)]), (wk, qkv_all.at[y, :, pl.ds(1024, 256)]),
            (wv, qkv_all.at[y, :, pl.ds(1280, 256)]), (wo, wo_all.at[y]), (wd, wd_all.at[y]),
        ]
    ):
        own.append(pltpu.make_async_copy(src, dst, own_sem.at[k]))
        own[-1].start()
    gain_all[y] = jnp.zeros((8, 256), F32)
    for i, n in enumerate(GAIN_SIZES):
        gain_all[y, pl.ds(i, 1), pl.ds(0, n)] = gain_ins[i][...].astype(F32)
    net.barrier()
    for cp in own:
        cp.wait()

    rows = pl.ds(pl.multiple_of(c * 80, 16), 80)

    def block(yq, start, n):
        return gu.at[yq, rows, pl.ds(pl.multiple_of(start, 128), n)]

    def gate_one(yq, xj, zj):
        return block(yq, (zj * 4 + xj) * 128, 128)

    def up_one(yq, xj, zj):
        return block(yq, 2048 + (xj * 4 + zj) * 128, 128)

    def qkv_piece(yq, half=None):
        off, n = {None: (0, 1536), 0: (0, 768), 1: (768, 768)}[half]
        return qkv_all.at[yq, rows, pl.ds(off, n)]

    def gu_piece(yq):
        return gu.at[yq, rows]

    def row_piece(ref, size):
        def piece(yq, half=None):
            off, n = {None: (0, size), 0: (0, size // 2), 1: (size // 2, size // 2)}[half]
            return ref.at[yq, pl.ds(pl.multiple_of(c * size + off, 16), n)]

        return piece

    wo_piece, wd_piece = row_piece(wo_all, 128), row_piece(wd_all, 256)
    gu_y = [Gather(net, "y", lambda j: gate_one(j, x, z)), Gather(net, "y", lambda j: up_one(j, x, z))]
    for g in gu_y:
        g.start()
    qkv = Relay(net, "y", qkv_piece, [(qkv_piece(y), qkv_piece(y))])
    w_o = Relay(net, "y", wo_piece, [(wo_piece(y), wo_piece(y))])
    w_d = Relay(net, "y", wd_piece, [(wd_piece(y), wd_piece(y))])
    qkv.start()
    gain_own = gain_all.at[y]
    gain_copies = [net.copy(gain_own, gain_own, "y", s) for s in STEPS]
    for g in gu_y:
        g.end()
    gu_1, gu_2 = [], []
    for s in (1, -1, 2):
        yq = net.at("y", s)
        gu_1.append(Gather(net, "x", lambda j, yq=yq: gate_one(yq, j, z)))
        gu_1.append(Gather(net, "z", lambda j, yq=yq: up_one(yq, x, j)))
        gu_2.append(Gather(net, "z", lambda j, yq=yq: block(yq, j * 512, 512)))
        gu_2.append(Gather(net, "x", lambda j, yq=yq: block(yq, 2048 + j * 512, 512)))
    for g in gu_1:
        g.start()
    for cp in gain_copies:
        cp.wait_recv()
    all_gains = gain_all[...]

    def gain(i, n):
        return jnp.concatenate([all_gains[yq, i : i + 1, :n] for yq in range(4)], axis=1)

    gains[0:1, :] = gain(0, 160)
    for i in range(3, 6):
        gains[i : i + 1, :] = gain(i, 160)
    gains[1:2, 0:256] = gain(1, 64)
    gains[2:3, 0:256] = gain(2, 64)
    g_in, g_q, g_k = gains[0:1, :], gains[1:2, 0:256], gains[2:3, 0:256]
    g_post, g_pre, g_fpost = gains[3:4, :], gains[4:5, :], gains[5:6, :]
    t = tokens[...].astype(F32)
    normed_low = (t * rms(t) * g_in).astype(BF)
    normed[own_rows, :] = normed_low

    def share(ref):
        return net.copy(ref.at[own_rows], ref.at[other_rows], "c")

    swaps = {}

    def swap(name, piece, j):
        swaps.setdefault(name, []).append(net.copy(piece(j), piece(j), "c"))

    def swapped(name):
        for cp in swaps[name]:
            cp.wait_recv()

    qkv.mid()
    w_o.start()
    w_d.start()
    swap("qkv", qkv_piece, net.at("y", 1))
    swap("qkv", qkv_piece, net.at("y", -1))
    for a, b in zip(gu_1, gu_2):
        a.end()
    for b in gu_2:
        b.start()
    qkv.end()
    swap("qkv", qkv_piece, net.at("y", 2))
    swapped("qkv")
    both = dot(normed_low, qkv_all[:, :, pl.ds(1024, 512)].reshape(640, 512))
    u = both[:, 0:256]
    raw[:, pl.ds(1024, 256)] = u
    k_all[c, z, x] = rope(u * rms(u) * g_k, cos[...], sin[...]).astype(BF)
    v_all[c, z, x] = both[:, 256:512].astype(BF)
    kx = Gather(net, "x", lambda j: k_all.at[c, z, j])
    vz = Gather(net, "z", lambda j: v_all.at[c, j, x])
    kz = Gather(net, "z", lambda j: k_all.at[c, j])
    vx = Gather(net, "x", lambda j: v_all.at[c, :, j])
    kx.start()
    vz.start()
    both = dot(normed_low, qkv_all[:, :, pl.ds(0, 1024)].reshape(640, 1024))
    raw[:, pl.ds(0, 1024)] = both
    for h in range(4):
        u = both[:, h * 256 : h * 256 + 256]
        q_s[pl.ds(h * 128, 128), :] = (rope(u * rms(u) * g_q, cos[...], sin[...]).astype(BF) * 0.0625).astype(BF)

    def swap_k(j):
        swap("kv", lambda j: k_all.at[c, j], j)

    def swap_v(j):
        swap("kv", lambda j: v_all.at[c, :, j], j)

    kx.end()
    kz.start()
    vz.end()
    vx.start()
    swap_k(z)
    swap_v(x)
    acc[...] = jnp.zeros_like(acc)
    inv_s[...] = jnp.zeros_like(inv_s)
    gain_s[...] = jnp.zeros_like(gain_s)
    ge[:, pl.ds(E_END, E_ROWS - E_END), :] = jnp.zeros((4, E_ROWS - E_END, 128), BF)
    gm[:, pl.ds(M_END, M_ROWS - M_END), :] = jnp.zeros((4, M_ROWS - M_END, 128), BF)
    gl[:, pl.ds(L_END, L_ROWS - L_END), :] = jnp.zeros((4, L_ROWS - L_END, 128), BF)
    shared = {"normed": share(normed)}
    w_o.mid()
    w_d.mid()
    for name, piece in (("wo", wo_piece), ("wd", wd_piece)):
        swap(name, piece, net.at("y", 1))
        swap(name, piece, net.at("y", -1))
    for g in gu_2:
        g.end()
    for s in (1, -1, 2):
        swap("gu", gu_piece, net.at("y", s))
    kz.end(swap_k)
    vx.end(swap_v)
    for r, name, piece in ((w_o, "wo", wo_piece), (w_d, "wd", wd_piece)):
        r.end()
        swap(name, piece, net.at("y", 2))
    swapped("kv")

    def fwd_tile(cc, j, diagonal):
        p = jnp.exp(dot_back(q_s[...], k_all[cc, j].reshape(512, 256)))
        if diagonal:
            p = jnp.where(causal(net, cc), p, 0.0)
        inv_s[...] += jnp.sum(p, axis=1, keepdims=True)
        acc[...] += dot(p.astype(BF), v_all[cc, j].reshape(512, 256))

    def fwd_step(i, _):
        fwd_tile(lax.rem(i, 2), lax.div(i, 2), False)
        return 0

    def fwd_last(i, _):
        fwd_tile(i, z, True)
        return 0

    lax.fori_loop(0, z * 2, fwd_step, 0)
    lax.fori_loop(0, 2, fwd_last, 0)
    inv = 1.0 / inv_s[...]
    inv_s[...] = inv
    acc[...] = acc[...] * inv
    for h in range(4):
        attn[own_rows, pl.ds(h * 256, 256)] = acc[pl.ds(h * 128, 128), :].astype(BF)
    shared["attn"] = share(attn)

    def put_gain(i, value):
        n = value.shape[1] // 4
        for yq in range(4):
            v = value[:, yq * n : yq * n + n]
            gain_s[yq, pl.ds(2 * i, 1), pl.ds(0, min(n, 128))] = v[:, :128]
            if n > 128:
                gain_s[yq, pl.ds(2 * i + 1, 1), pl.ds(0, n - 128)] = v[:, 128:]

    swapped("wo")
    w_out = wo_all[...].reshape(1024, 640)
    proj = dot(attn[own_rows, :], w_out)
    r_proj = rms(proj)
    hidden = tokens[...].astype(F32) + proj * r_proj * g_post
    r_hidden = rms(hidden)
    ffn_low = (hidden * r_hidden * g_pre).astype(BF)
    ffn[own_rows, :] = ffn_low
    shared["ffn"] = share(ffn)
    swapped("gu")
    for i in range(4):
        cs, cs2 = pl.ds(i * 512, 512), pl.ds(2048 + i * 512, 512)
        gate = dot(ffn_low, gu[:, :, cs].reshape(640, 512))
        up = dot(ffn_low, gu[:, :, cs2].reshape(640, 512))
        t = jnp.tanh(C_ROOT * (gate + C_CUBE * gate * gate * gate))
        gelu = 0.5 * gate * (1.0 + t)
        slope = 0.5 * (1.0 + t) + 0.5 * gate * (1.0 - t * t) * (C_ROOT * (1.0 + 3.0 * C_CUBE * gate * gate))
        mixed[own_rows, cs] = (gelu * up).astype(BF)
        f_s[:, cs] = up * slope
        g_s[:, cs] = gelu
    shared["mixed"] = share(mixed)
    swapped("wd")
    down = dot(mixed[own_rows, :], wd_all[...].reshape(2048, 640))
    r_down = rms(down)
    layer_out[...] = (hidden + down * r_down * g_fpost).astype(BF)
    out_grad = cot[...].astype(F32)
    down_grad = norm_back(down, r_down, g_fpost, out_grad).astype(BF)
    put_gain(5, gain_grad(down, r_down, out_grad))
    downg[own_rows, :] = down_grad
    shared["downg"] = share(downg)
    for i in range(4):
        cs, cs2 = pl.ds(i * 512, 512), pl.ds(2048 + i * 512, 512)
        mg = dot_back(down_grad, wd_all[i])
        gug[own_rows, cs] = (mg * f_s[:, cs]).astype(BF)
        gug[own_rows, cs2] = (mg * g_s[:, cs]).astype(BF)
    shared["gug"] = share(gug)
    ffn_grad = dot_back(gug[own_rows, :], gu[...].reshape(640, 4096))
    hidden_grad = out_grad + norm_back(hidden, r_hidden, g_pre, ffn_grad)
    put_gain(4, gain_grad(hidden, r_hidden, ffn_grad))
    hidden_grad_s[...] = hidden_grad
    proj_grad = norm_back(proj, r_proj, g_post, hidden_grad).astype(BF)
    put_gain(3, gain_grad(proj, r_proj, hidden_grad))
    projg[own_rows, :] = proj_grad
    shared["projg"] = share(projg)
    attn_grad = dot_back(proj_grad, w_out).astype(BF)
    for h in range(4):
        do_s[pl.ds(h * 128, 128), :] = attn_grad[:, h * 256 : h * 256 + 256]
    delta_s[...] = jnp.sum(do_s[...].astype(F32) * acc[...], axis=1, keepdims=True)

    def cols(start, width):
        return pl.ds(pl.multiple_of(start, 128), width)

    def put(g, off, n, value, col_blocks):
        value = value.astype(BF)
        for yq in range(4):
            for j in range(col_blocks):
                g[yq, pl.ds(off + j * n, n), :] = value[yq * n : yq * n + n, j * 128 : j * 128 + 128]

    for name in ("attn", "ffn", "mixed", "downg", "gug", "projg"):
        shared[name].wait_recv()
    for part in range(2):
        put(ge, OFF_G + part * 640, 160, tdot(ffn[...], gug[:, cols(c * 1024 + part * 512, 512)]), 4)
        put(ge, OFF_U + part * 640, 160, tdot(ffn[...], gug[:, cols(2048 + c * 1024 + part * 512, 512)]), 4)
    early_a = Group(net, ge, e_full, EA_PARTS, group_b[0])
    early_a.step()
    for yq in range(4):
        value = tdot(attn[:, cols(yq * 256 + c * 128, 128)], projg[...]).astype(BF)
        for j in range(5):
            ge[yq, pl.ds(OFF_O + j * 128, 128), :] = value[:, j * 128 : j * 128 + 128]
        value = tdot(mixed[:, cols(yq * 512 + c * 256, 256)], downg[...]).astype(BF)
        for j in range(5):
            ge[yq, pl.ds(OFF_D + j * 256, 256), :] = value[:, j * 128 : j * 128 + 128]
    early_b = Group(net, ge, e_full, EB_PARTS, group_b[1])
    early_b.step()

    acc[...] = jnp.zeros_like(acc)

    def tile(cc, j, diagonal):
        kt, vt = k_all[cc, j].reshape(512, 256), v_all[cc, j].reshape(512, 256)
        p = jnp.exp(dot_back(q_s[...], kt)) * inv_s[...]
        if diagonal:
            p = jnp.where(causal(net, cc), p, 0.0)
        ds = (p * (dot_back(do_s[...], vt) - delta_s[...])).astype(BF)
        acc[...] += dot(ds, kt)
        dk[cc, j] = tdot(ds, q_s[...]).astype(BF).reshape(4, 128, 256)
        dv[cc, j] = tdot(p.astype(BF), do_s[...]).astype(BF).reshape(4, 128, 256)

    kc, vc = {}, {}

    def tiles(s):
        j = net.at("z", s)

        def step(i, _):
            cc = lax.rem(other + i, 2)
            if s == 0:
                tile(cc, j, True)
            else:

                @pl.when(j < z)
                def _():
                    tile(cc, j, False)

                @pl.when(j > z)
                def _():
                    dk[cc, j] = jnp.zeros((4, 128, 256), BF)
                    dv[cc, j] = jnp.zeros((4, 128, 256), BF)

            return 0

        lax.fori_loop(0, 2, step, 0)
        kc[s] = net.copy(dk.at[other, j], kin.at[j], "c")
        vc[s] = net.copy(dv.at[other, j], vin.at[j], "c")

    k1 = Scatter(net, "z", lambda j: kin.at[j], kbufs)
    v1 = Scatter(net, "x", lambda j: vin.at[:, j], vbufs)
    k2 = Scatter(net, "x", lambda j: kin.at[z, j], k2bufs)
    v2 = Scatter(net, "z", lambda j: vin.at[j, x], v2bufs)

    def take(s):
        j = net.at("z", s)
        kc[s].wait_recv()
        add_rows(kin.at[j], (dk.at[c, j],))
        if s != 0:
            k1.send(s)
        vc[s].wait_recv()
        add_rows(vin.at[j], (dv.at[c, j],))

    tiles(2)
    tiles(1)
    take(2)
    tiles(-1)
    take(1)
    tiles(0)
    take(-1)
    take(0)
    v1.start()

    total_q = jnp.zeros((1, 256), F32)
    for h in range(4):
        v = raw[:, pl.ds(h * 256, 256)]
        r = rms(v)
        u = rope_back(acc[pl.ds(h * 128, 128), :] * 0.0625, cos[...], sin[...])
        total_q += gain_grad(v, r, u)
        qkvg[own_rows, pl.ds(h * 256, 256)] = norm_back(v, r, g_q, u).astype(BF)
    put_gain(1, total_q)
    q_cols, kv_cols = pl.ds(0, 1024), pl.ds(1024, 512)
    share_q = net.copy(qkvg.at[own_rows, q_cols], qkvg.at[other_rows, q_cols], "c")
    normed_grad = dot_back(qkvg[own_rows, q_cols], qkv_all[:, :, q_cols].reshape(640, 1024))
    early_b.step()
    shared["normed"].wait_recv()
    share_q.wait_recv()
    put(gm, OFF_Q, 160, tdot(normed[...], qkvg[:, cols(c * 512, 512)]), 4)
    middle = Group(net, gm, m_full, M_PARTS, group_b[2])
    k1.end()
    k2.start()
    v1.end()
    v2.start()
    middle.step()
    early_b.step()
    k2.end()
    v2.end()

    v = raw[:, pl.ds(1024, 256)]
    r = rms(v)
    u = rope_back(kin[z, x].astype(F32), cos[...], sin[...])
    put_gain(2, gain_grad(v, r, u))
    qkvg[own_rows, pl.ds(1024, 256)] = norm_back(v, r, g_k, u).astype(BF)
    qkvg[own_rows, pl.ds(1280, 256)] = vin[z, x]
    share_kv = net.copy(qkvg.at[own_rows, kv_cols], qkvg.at[other_rows, kv_cols], "c")
    normed_grad = normed_grad + dot_back(qkvg[own_rows, kv_cols], qkv_all[:, :, kv_cols].reshape(640, 512))
    t = tokens[...].astype(F32)
    r = rms(t)
    put_gain(0, gain_grad(t, r, normed_grad))
    gain_copy = net.copy(gain_s, gain_other, "c")
    input_grad[...] = hidden_grad_s[...] + norm_back(t, r, g_in, normed_grad)
    middle.step()
    share_kv.wait_recv()
    put(gl, OFF_K, 160, tdot(normed[...], qkvg[:, cols(1024 + c * 128, 128)]), 1)
    put(gl, OFF_V, 160, tdot(normed[...], qkvg[:, cols(1280 + c * 128, 128)]), 1)
    gain_copy.wait_recv()
    gl[:, pl.ds(OFF_GAIN, 16), :] = (gain_s[...] + gain_other[...]).astype(BF)
    late = Group(net, gl, l_full, L_PARTS, group_b[3])
    late.step()
    early_a.step()
    early_b.step()
    middle.step()
    late.step()
    early_a.step()
    early_b.step()
    middle.step()
    late.step()
    early_a.step()
    early_b.step()
    middle.step()
    late.step()
    early_a.step()
    middle.step()
    late.step()
    early_a.step()
    late.step()
    early_b.step()
    middle.step()
    early_a.step()
    late.step()
    net.drain()


def layer(*args):
    def s(dtype, *shape):
        return jax.ShapeDtypeStruct(shape, dtype)

    n = 6 + 4 + 3 + 18 + 18 + 3 + 4 + 4 + 3 + 3 + 3 + 12 + 8 + 8 + 2 + 8 + 12 + sum(16 * len(p) + 1 for p in ALL_PARTS)
    big, small = VMEM((4, 128, 256), BF), VMEM((128, 256), BF)
    whole = VMEM((2, 4, 4, 128, 256), BF)
    column = VMEM((512, 1), F32)
    return pl.pallas_call(
        layer_kernel,
        out_shape=(
            s(BF, 128, 640), s(F32, 128, 640), s(BF, 2, E_ROWS, 128), s(BF, 2, M_ROWS, 128), s(BF, 2, L_ROWS, 128)
        ),
        in_specs=[ANYSPEC] * 7 + [VSPEC] * 10,
        out_specs=[VSPEC] * 5,
        scratch_shapes=[
            VMEM((4, 160, 1536), BF), VMEM((4, 160, 4096), BF), VMEM((4, 256, 640), BF), VMEM((4, 512, 640), BF),
            whole, whole,
            *[VMEM((256, n), BF) for n in (640, 1536, 1024, 640, 640, 4096, 2048, 640)],
            VMEM((4, 8, 256), F32), VMEM((8, 640), F32), VMEM((4, 16, 128), F32), VMEM((4, 16, 128), F32),
            VMEM((4, E_ROWS, 128), BF), VMEM((4, M_ROWS, 128), BF), VMEM((4, L_ROWS, 128), BF),
            whole, whole, VMEM((4, 4, 128, 256), BF), VMEM((4, 4, 128, 256), BF),
            VMEM((512, 256), F32), column, column, VMEM((512, 256), BF), VMEM((512, 256), BF), VMEM((128, 1280), F32),
            VMEM((128, 2048), F32), VMEM((128, 2048), F32), VMEM((128, 640), F32),
            *[big] * 6, *[small] * 6,
            *[b for parts in ALL_PARTS for b in group_bufs(parts)],
            pltpu.SemaphoreType.DMA((n,)),
            pltpu.SemaphoreType.DMA((n,)),
            pltpu.SemaphoreType.DMA((7,)),
        ],
        compiler_params=pltpu.CompilerParams(collective_id=0, has_side_effects=True, vmem_limit_bytes=VMEM_LIMIT),
        name="layer",
    )(*args)


def unpack_kernel(e, m, l, oq, ok, ov, oo, og, ou, od, *gain_outs):
    for c in range(2):

        def block(full, off, n, j):
            return full[c, pl.ds(off + j * n, n), :].astype(F32)

        for j in range(4):
            oq[:, pl.ds(c * 512 + j * 128, 128)] = block(m, OFF_Q, 160, j)
        ok[:, pl.ds(c * 128, 128)] = block(l, OFF_K, 160, 0)
        ov[:, pl.ds(c * 128, 128)] = block(l, OFF_V, 160, 0)
        for j in range(8):
            og[:, pl.ds(c * 1024 + j * 128, 128)] = block(e, OFF_G, 160, j)
            ou[:, pl.ds(c * 1024 + j * 128, 128)] = block(e, OFF_U, 160, j)
        for j in range(5):
            oo[pl.ds(c * 128, 128), pl.ds(j * 128, 128)] = block(e, OFF_O, 128, j)
            od[pl.ds(c * 256, 256), pl.ds(j * 128, 128)] = block(e, OFF_D, 256, j)
    rows = l[0, pl.ds(OFF_GAIN, 16), :].astype(F32)
    for i, n in enumerate(GAIN_SIZES):
        gain_outs[i][:, pl.ds(0, min(n, 128))] = rows[2 * i : 2 * i + 1, : min(n, 128)]
        if n > 128:
            gain_outs[i][:, pl.ds(128, n - 128)] = rows[2 * i + 1 : 2 * i + 2, : n - 128]


def unpack(e, m, l):
    def s(*shape):
        return jax.ShapeDtypeStruct(shape, F32)

    return pl.pallas_call(
        unpack_kernel,
        out_shape=(
            s(160, 1024), s(160, 256), s(160, 256), s(256, 640), s(160, 2048), s(160, 2048), s(512, 640),
            *[s(1, n) for n in GAIN_SIZES],
        ),
        in_specs=[VSPEC] * 3,
        out_specs=[VSPEC] * 13,
        compiler_params=pltpu.CompilerParams(vmem_limit_bytes=VMEM_LIMIT),
        name="unpack",
    )(e, m, l)


def local(
    tokens, positions, w_query, w_key, w_value, w_out, w_gate, w_up, w_down,
    gain_in, gain_query, gain_key, gain_attn_post, gain_ffn_pre, gain_ffn_post, cotangent,
):
    gains = [
        g.reshape(1, g.shape[0]) for g in (gain_in, gain_query, gain_key, gain_attn_post, gain_ffn_pre, gain_ffn_post)
    ]
    exponents = jnp.arange(0, 256, 2, dtype=F32) / 256
    inverse = 1.0 / ROPE_BASE**exponents
    angles = positions.astype(F32)[:, None] * inverse[None, :]
    cos, sin = jnp.cos(angles), jnp.sin(angles)
    layer_out, input_grad, e_full, m_full, l_full = layer(
        w_query, w_key, w_value, w_out, w_gate, w_up, w_down, *gains, tokens, cotangent, cos, sin
    )
    oq, ok, ov, oo, og, ou, od, *gain_grads = unpack(e_full, m_full, l_full)
    return (layer_out, input_grad, oq, ok, ov, oo, og, ou, od, *[g.reshape(g.shape[1]) for g in gain_grads])


def solution(mesh):
    rows, both, vec = P("fsdp", None), P(("fsdp", "ctx"), None), P("fsdp")
    in_specs = (both, P(("fsdp", "ctx")), *[rows] * 7, *[vec] * 6, both)
    out_specs = (both, both, *[rows] * 7, *[vec] * 6)
    return jax.shard_map(local, mesh=mesh, in_specs=in_specs, out_specs=out_specs, check_vma=False)
```

time: 656 us -> 148 us (0.23)
  waiting for transfers between devices: 444 us -> 0 us
  Pallas kernels: 0 us -> 139 us
  blocking collectives: 81.4 us -> 0 us
  matrix products: 42.2 us -> 0 us
  other arithmetic: 37.5 us -> 1.63 us
  local copies, waits for them, and re-layouts: 29 us -> 6.28 us
  between operations: 17.6 us -> 0.68 us
    reduce_scatter x5 -> x0, waiting for transfers between devices: 253 us -> none  [the longest x3 192 us: sent_together(): whole = lax.psum_scatter(both, axis, scatter_dimension=dim, tiled=True)]
    all_gather x5 -> x0, waiting for transfers between devices: 156 us -> none  [the longest x3 113 us: side_by_side(): whole = lax.all_gather(both, axis, axis=dim, tiled=True)]
    pallas_call x0 -> x2, Pallas kernels: none -> 139 us  [the longest x1 135 us: layer(): pl.pallas_call(layer_kernel, out_shape=(s(BF, 128, 640), s(F32, 128, 640)...]
    psum x1 -> x0, blocking collectives: 64.9 us -> none  [local(): lax.psum(attn_shares[4].astype(jnp.bfloat16), 'ctx').astype(jnp.float32)]
    dot_general x28 -> x0, matrix products: 42.2 us -> none  [the longest x10 13.6 us: dot_back(): lax.dot_general(left_side, right_side, (((1,), (1,)), ((), ())), preferre...]
    psum x1 -> x0, waiting for transfers between devices: 33.5 us -> none  [local(): lax.psum(attn_shares[0].astype(jnp.bfloat16), 'ctx').astype(jnp.float32)]
    convert_element_type x27 -> x1, other arithmetic: 18.3 us -> 0.66 us  [local(): angles = positions.astype(F32)[:, None] * inverse[None, :]]
    unnamed x2 -> x0, blocking collectives: 16.5 us -> none
  transfers between devices with their start and end apart: 11 -> 0, of which waited for: 11 -> 0; matrix products, arithmetic and copies ran while one was open for 9% -> 0% of each run, Pallas kernels for 0% -> 0%
where the time goes in v2:
time: 148 us
  Pallas kernels  139 us (94%)
  local copies, waits for them, and re-layouts  6.28 us (4%)
  other arithmetic  1.63 us (1%)
    pallas_call x1, Pallas kernels, layer(): pl.pallas_call(layer_kernel, out_shape=(s(BF, 128, 640), s(F32, 128, 640)...  135 us
    reshape x4, local copies, waits for them, and re-layouts, local(): g.reshape(1, g.shape[0])  4.88 us
    pallas_call x1, Pallas kernels, unpack(): pl.pallas_call(unpack_kernel, out_shape=(s(160, 1024), s(160, 256), s(160...  4.47 us

profile of v2, /device:TPU:1, one launch (start us, length us, event | category | flops | bytes accessed | tf_op | source)
XLA Modules:
  0.0 147.6 jit_solution(18056944232605131604)
XLA Ops:
  0.6 0.7 convert_element_type.3
  1.3 1.2 reshape.73.refs_7_
  2.5 1.2 reshape.76.refs_10_
  3.8 1.2 reshape.77.refs_11_
  5.0 1.2 reshape.78.refs_12_
  6.2 1.0 multiply_sine_fusion
  7.2 134.5 %layer.1 = (bf16[128,640]{1,0:T(8,128)(2,1)}, f32[128,640]{1,0:T(8,128)}, bf16[2,4608,128]{2,1,0:T(8,128)(2,1)}, bf16[2,768,128]{2,1,0:T(8,128)(2,1)}, bf16[2,512,128]{2,1,0:T(8,128)(2,1)}) custom-call(bf16[160,1024]{1,0:T(8,128)(2,1)} %refs_0_.1, bf16[160,256]{1,0:T(8,128)(2,1)} %refs_1_.1, bf16[160,256]{1,0:T(8,128)(2,1)} %refs_2_.1, ...), custom_call_target="tpu_custom_call" | custom-call | tf_op jit(solution)/shard_map/layer/pallas_call | solution.py:724
  141.7 0.0 copy-start.1
  141.7 0.0 copy-start
  141.7 4.5 %unpack.1 = (f32[160,1024]{1,0:T(8,128)}, f32[160,256]{1,0:T(8,128)}, f32[160,256]{1,0:T(8,128)}, f32[256,640]{1,0:T(8,128)}, f32[160,2048]{1,0:T(8,128)}, /*ind...) custom-call(bf16[2,4608,128]{2,1,0:T(8,128)(2,1)} %get-tuple-element, ...), custom_call_target="tpu_custom_call" | custom-call | tf_op jit(solution)/shard_map/unpack/pallas_call | solution.py:778
  146.2 0.0 copy-done.1
  146.2 0.7 copy.33
  146.9 0.0 copy-done
  146.9 0.7 copy.34
  (1 shorter events, 0.0 us)
Async XLA Ops:
  141.7 4.5 %copy-start.1 = (bf16[128,640]{1,0:T(8,128)(2,1)S(1)}, bf16[128,640]{1,0:T(8,128)(2,1)}, u32[]{:S(2)}) copy-start(bf16[128,640]{1,0:T(8,128)(2,1)} %get-tuple-element.68) | copy-start | bytes 491524
  141.7 5.2 %copy-start = (f32[128,640]{1,0:T(8,128)S(1)}, f32[128,640]{1,0:T(8,128)}, u32[]{:S(2)}) copy-start(f32[128,640]{1,0:T(8,128)} %get-tuple-element.69) | copy-start | bytes 983044

commit v3 on v2

--- a/solution.py
+++ b/solution.py
@@ -23,7 +23,7 @@
 OFF_G, OFF_U, OFF_O, OFF_D, E_END = 0, 1280, 2560, 3200, 4480
 OFF_Q, M_END = 0, 640
 OFF_K, OFF_V, OFF_GAIN, L_END = 0, 160, 320, 336
-EA_PARTS = ((0, 2560, "yzx"),)
+EA_PARTS = ((0, 1280, "yzx"), (1280, 1280, "yxz"))
 EB_PARTS = ((2560, 1024, "xzy"), (3584, 1024, "zxy"))
 M_PARTS = ((0, 256, "yzx"), (256, 256, "xzy"), (512, 256, "zxy"))
 L_PARTS = ((0, 256, "yzx"), (256, 256, "xyz"))
@@ -125,6 +125,36 @@
                 then(self.net.at(self.axis, -s))
 
 
+class RelayScatter:
+    def __init__(self, net, axis, q, bufs):
+        self.net, self.axis, self.q, self.bufs = net, axis, q, bufs
+        self.n = bufs[0].shape[1] // 2
+
+    def half(self, ref, h):
+        return ref.at[:, pl.ds(h * self.n, self.n)]
+
+    def start(self):
+        far = self.q(self.net.at(self.axis, 2))
+        first = self.bufs[0]
+        self.cl = self.net.copy(self.half(far, 0), self.half(first, 0), self.axis, 1)
+        self.ch = self.net.copy(self.half(far, 1), self.half(first, 1), self.axis, -1)
+
+    def mid(self):
+        up, down = self.q(self.net.at(self.axis, 1)), self.q(self.net.at(self.axis, -1))
+        first = self.bufs[0]
+        self.cl.wait_recv()
+        add_rows(self.half(up, 0), (self.half(first, 0),))
+        self.cp = self.net.copy(up, self.bufs[1], self.axis, 1)
+        self.ch.wait_recv()
+        add_rows(self.half(down, 1), (self.half(first, 1),))
+        self.cm = self.net.copy(down, self.bufs[2], self.axis, -1)
+
+    def end(self, out=None):
+        self.cp.wait_recv()
+        self.cm.wait_recv()
+        add_rows(self.q(self.net.pos(self.axis)), self.bufs[1:], out)
+
+
 class Scatter:
     def __init__(self, net, axis, q, bufs):
         self.net, self.axis, self.q, self.bufs = net, axis, q, bufs
@@ -213,7 +243,8 @@
 
 
 class Group:
-    def __init__(self, net, g, full, parts, bufs):
+    def __init__(self, net, g, full, parts, bufs, relay=False):
+        self.relay = relay
         self.net, self.g, self.full, self.parts, self.bufs = net, g, full, parts, bufs
         self.place = [[0, 4, off, rows] for off, rows, _ in parts]
         self.phase = -1
@@ -232,7 +263,8 @@
         self.runs = []
         for p, (_, _, order) in enumerate(self.parts):
             k = (p * 3 + phase) * 3
-            self.runs.append(Scatter(self.net, order[phase], self.q(p, order[phase]), self.bufs[k : k + 3]))
+            kind = RelayScatter if self.relay and phase == 0 else Scatter
+            self.runs.append(kind(self.net, order[phase], self.q(p, order[phase]), self.bufs[k : k + 3]))
             self.runs[-1].start()
 
     def scatter_end(self, phase):
@@ -245,6 +277,10 @@
                 self.place[p] = [y0, yn, r0 + self.net.pos(axis) * (rn // 4), rn // 4]
             _, _, r0, rn = self.place[p]
             r.end(self.full.at[pl.ds(self.net.c, 1), pl.ds(pl.multiple_of(r0, 16), rn)] if phase == 2 else None)
+
+    def mid(self):
+        for r in self.runs:
+            r.mid()
 
     def gather_start(self, stage):
         self.runs = []
@@ -329,7 +365,7 @@
         own[-1].start()
     gain_all[y] = jnp.zeros((8, 256), F32)
     for i, n in enumerate(GAIN_SIZES):
-        gain_all[y, pl.ds(i, 1), pl.ds(0, n)] = gain_ins[i][...].astype(F32)
+        gain_all[y, pl.ds(i, 1), pl.ds(0, n)] = gain_ins[i][...].astype(F32).reshape(1, n)
     net.barrier()
     for cp in own:
         cp.wait()
@@ -550,11 +586,6 @@
     put_gain(3, gain_grad(proj, r_proj, hidden_grad))
     projg[own_rows, :] = proj_grad
     shared["projg"] = share(projg)
-    attn_grad = dot_back(proj_grad, w_out).astype(BF)
-    for h in range(4):
-        do_s[pl.ds(h * 128, 128), :] = attn_grad[:, h * 256 : h * 256 + 256]
-    delta_s[...] = jnp.sum(do_s[...].astype(F32) * acc[...], axis=1, keepdims=True)
-
     def cols(start, width):
         return pl.ds(pl.multiple_of(start, 128), width)
 
@@ -564,13 +595,20 @@
             for j in range(col_blocks):
                 g[yq, pl.ds(off + j * n, n), :] = value[yq * n : yq * n + n, j * 128 : j * 128 + 128]
 
-    for name in ("attn", "ffn", "mixed", "downg", "gug", "projg"):
+    for name in ("ffn", "gug"):
         shared[name].wait_recv()
     for part in range(2):
         put(ge, OFF_G + part * 640, 160, tdot(ffn[...], gug[:, cols(c * 1024 + part * 512, 512)]), 4)
         put(ge, OFF_U + part * 640, 160, tdot(ffn[...], gug[:, cols(2048 + c * 1024 + part * 512, 512)]), 4)
-    early_a = Group(net, ge, e_full, EA_PARTS, group_b[0])
+    early_a = Group(net, ge, e_full, EA_PARTS, group_b[0], relay=True)
     early_a.step()
+    attn_grad = dot_back(proj_grad, w_out).astype(BF)
+    for h in range(4):
+        do_s[pl.ds(h * 128, 128), :] = attn_grad[:, h * 256 : h * 256 + 256]
+    delta_s[...] = jnp.sum(do_s[...].astype(F32) * acc[...], axis=1, keepdims=True)
+
+    for name in ("attn", "mixed", "downg", "projg"):
+        shared[name].wait_recv()
     for yq in range(4):
         value = tdot(attn[:, cols(yq * 256 + c * 128, 128)], projg[...]).astype(BF)
         for j in range(5):
@@ -638,6 +676,7 @@
     take(2)
     tiles(-1)
     take(1)
+    early_a.mid()
     tiles(0)
     take(-1)
     take(0)
@@ -667,6 +706,7 @@
     early_b.step()
     k2.end()
     v2.end()
+    early_a.step()
 
     v = raw[:, pl.ds(1024, 256)]
     r = rms(v)
@@ -708,7 +748,6 @@
     late.step()
     early_b.step()
     middle.step()
-    early_a.step()
     late.step()
     net.drain()
 
@@ -748,7 +787,9 @@
     )(*args)
 
 
-def unpack_kernel(e, m, l, oq, ok, ov, oo, og, ou, od, *gain_outs):
+def unpack_kernel(e, m, l, lo, ig, lo_out, ig_out, oq, ok, ov, oo, og, ou, od, *gain_outs):
+    lo_out[...] = lo[...]
+    ig_out[...] = ig[...]
     for c in range(2):
 
         def block(full, off, n, j):
@@ -771,30 +812,28 @@
             gain_outs[i][:, pl.ds(128, n - 128)] = rows[2 * i + 1 : 2 * i + 2, : n - 128]
 
 
-def unpack(e, m, l):
+def unpack(e, m, l, lo, ig):
     def s(*shape):
         return jax.ShapeDtypeStruct(shape, F32)
 
     return pl.pallas_call(
         unpack_kernel,
         out_shape=(
-            s(160, 1024), s(160, 256), s(160, 256), s(256, 640), s(160, 2048), s(160, 2048), s(512, 640),
+            jax.ShapeDtypeStruct((128, 640), BF), s(128, 640), s(160, 1024), s(160, 256), s(160, 256), s(256, 640), s(160, 2048), s(160, 2048), s(512, 640),
             *[s(1, n) for n in GAIN_SIZES],
         ),
-        in_specs=[VSPEC] * 3,
-        out_specs=[VSPEC] * 13,
+        in_specs=[VSPEC] * 5,
+        out_specs=[VSPEC] * 15,
         compiler_params=pltpu.CompilerParams(vmem_limit_bytes=VMEM_LIMIT),
         name="unpack",
-    )(e, m, l)
+    )(e, m, l, lo, ig)
 
 
 def local(
     tokens, positions, w_query, w_key, w_value, w_out, w_gate, w_up, w_down,
     gain_in, gain_query, gain_key, gain_attn_post, gain_ffn_pre, gain_ffn_post, cotangent,
 ):
-    gains = [
-        g.reshape(1, g.shape[0]) for g in (gain_in, gain_query, gain_key, gain_attn_post, gain_ffn_pre, gain_ffn_post)
-    ]
+    gains = (gain_in, gain_query, gain_key, gain_attn_post, gain_ffn_pre, gain_ffn_post)
     exponents = jnp.arange(0, 256, 2, dtype=F32) / 256
     inverse = 1.0 / ROPE_BASE**exponents
     angles = positions.astype(F32)[:, None] * inverse[None, :]
@@ -802,7 +841,7 @@
     layer_out, input_grad, e_full, m_full, l_full = layer(
         w_query, w_key, w_value, w_out, w_gate, w_up, w_down, *gains, tokens, cotangent, cos, sin
     )
-    oq, ok, ov, oo, og, ou, od, *gain_grads = unpack(e_full, m_full, l_full)
+    layer_out, input_grad, oq, ok, ov, oo, og, ou, od, *gain_grads = unpack(e_full, m_full, l_full, layer_out, input_grad)
     return (layer_out, input_grad, oq, ok, ov, oo, og, ou, od, *[g.reshape(g.shape[1]) for g in gain_grads])
 
 

time: 148 us -> 136 us (0.919)
  local copies, waits for them, and re-layouts: 6.28 us -> 0 us
  Pallas kernels: 139 us -> 133 us
    pallas_call x1, Pallas kernels: 135 us -> 128 us  [layer(): pl.pallas_call(layer_kernel, out_shape=(s(BF, 128, 640), s(F32, 128, 640)...]
    reshape x4 -> x0, local copies, waits for them, and re-layouts: 4.88 us -> none  [local(): g.reshape(1, g.shape[0])]
where the time goes in v3:
time: 136 us
  Pallas kernels  133 us (98%)
  other arithmetic  1.64 us (1%)
    pallas_call x1, Pallas kernels, layer(): pl.pallas_call(layer_kernel, out_shape=(s(BF, 128, 640), s(F32, 128, 640)...  128 us
    pallas_call x1, Pallas kernels, unpack(): pl.pallas_call(unpack_kernel, out_shape=(jax.ShapeDtypeStruct((128, 640),...  4.76 us

profile of v3, /device:TPU:1, one launch (start us, length us, event | category | flops | bytes accessed | tf_op | source)
XLA Modules:
  0.0 135.7 jit_solution(1037467697364576306)
XLA Ops:
  0.6 0.7 convert_element_type.3
  1.3 1.0 multiply_sine_fusion
  2.3 128.4 %layer.1 = (bf16[128,640]{1,0:T(8,128)(2,1)}, f32[128,640]{1,0:T(8,128)}, bf16[2,4608,128]{2,1,0:T(8,128)(2,1)}, bf16[2,768,128]{2,1,0:T(8,128)(2,1)}, bf16[2,512,128]{2,1,0:T(8,128)(2,1)}) custom-call(bf16[160,1024]{1,0:T(8,128)(2,1)} %refs_0_.1, bf16[160,256]{1,0:T(8,128)(2,1)} %refs_1_.1, bf16[160,256]{1,0:T(8,128)(2,1)} %refs_2_.1, ...), custom_call_target="tpu_custom_call" | custom-call | tf_op jit(solution)/shard_map/layer/pallas_call | solution.py:763
  130.7 4.8 %unpack.1 = (bf16[128,640]{1,0:T(8,128)(2,1)}, f32[128,640]{1,0:T(8,128)}, f32[160,1024]{1,0:T(8,128)}, f32[160,256]{1,0:T(8,128)}, f32[160,256]{1,0:T(8,128)}, ...) custom-call(bf16[2,4608,128]{2,1,0:T(8,128)(2,1)} %get-tuple-element, ...), custom_call_target="tpu_custom_call" | custom-call | tf_op jit(solution)/shard_map/unpack/pallas_call | solution.py:819
  (1 shorter events, 0.0 us)

commit v4 on v3

--- a/solution.py
+++ b/solution.py
@@ -340,11 +340,13 @@
 
     wq, wk, wv, wo, wg, wu, wd = take_refs(7)
     gain_ins = take_refs(6)
-    tokens, cot, cos, sin = take_refs(4)
-    layer_out, input_grad, e_full, m_full, l_full = take_refs(5)
+    tokens, cot, positions, inverse = take_refs(4)
+    layer_out, input_grad, e_out, m_out, l_full = take_refs(5)
+    e_full, m_full = take_refs(2)
     qkv_all, gu, wo_all, wd_all, k_all, v_all = take_refs(6)
     normed, qkvg, attn, projg, ffn, gug, mixed, downg = take_refs(8)
     gain_all, gains, gain_s, gain_other, ge, gm, gl = take_refs(7)
+    cos, sin = take_refs(2)
     dk, dv, kin, vin, acc, inv_s, delta_s, do_s, q_s, raw, f_s, g_s, hidden_grad_s = take_refs(13)
     kbufs, vbufs, k2bufs, v2bufs = take_refs(3), take_refs(3), take_refs(3), take_refs(3)
     group_b = [take_refs(9 * len(parts)) for parts in ALL_PARTS]
@@ -430,6 +432,11 @@
     gains[2:3, 0:256] = gain(2, 64)
     g_in, g_q, g_k = gains[0:1, :], gains[1:2, 0:256], gains[2:3, 0:256]
     g_post, g_pre, g_fpost = gains[3:4, :], gains[4:5, :], gains[5:6, :]
+    ids = jnp.broadcast_to(positions[...].astype(F32).reshape(1, 128), (128, 128))
+    row, col = (lax.broadcasted_iota(jnp.int32, (128, 128), d) for d in (0, 1))
+    angles = jnp.sum(jnp.where(row == col, ids, 0.0), axis=1, keepdims=True) * inverse[...]
+    cos[...] = jnp.cos(angles)
+    sin[...] = jnp.sin(angles)
     t = tokens[...].astype(F32)
     normed_low = (t * rms(t) * g_in).astype(BF)
     normed[own_rows, :] = normed_low
@@ -747,8 +754,14 @@
     early_a.step()
     late.step()
     early_b.step()
+    e_copy = pltpu.make_async_copy(e_full, e_out, own_sem.at[0])
+    e_copy.start()
     middle.step()
+    m_copy = pltpu.make_async_copy(m_full, m_out, own_sem.at[1])
+    m_copy.start()
     late.step()
+    e_copy.wait()
+    m_copy.wait()
     net.drain()
 
 
@@ -766,13 +779,15 @@
             s(BF, 128, 640), s(F32, 128, 640), s(BF, 2, E_ROWS, 128), s(BF, 2, M_ROWS, 128), s(BF, 2, L_ROWS, 128)
         ),
         in_specs=[ANYSPEC] * 7 + [VSPEC] * 10,
-        out_specs=[VSPEC] * 5,
+        out_specs=[VSPEC, VSPEC, ANYSPEC, ANYSPEC, VSPEC],
         scratch_shapes=[
+            VMEM((2, E_ROWS, 128), BF), VMEM((2, M_ROWS, 128), BF),
             VMEM((4, 160, 1536), BF), VMEM((4, 160, 4096), BF), VMEM((4, 256, 640), BF), VMEM((4, 512, 640), BF),
             whole, whole,
             *[VMEM((256, n), BF) for n in (640, 1536, 1024, 640, 640, 4096, 2048, 640)],
             VMEM((4, 8, 256), F32), VMEM((8, 640), F32), VMEM((4, 16, 128), F32), VMEM((4, 16, 128), F32),
             VMEM((4, E_ROWS, 128), BF), VMEM((4, M_ROWS, 128), BF), VMEM((4, L_ROWS, 128), BF),
+            VMEM((128, 128), F32), VMEM((128, 128), F32),
             whole, whole, VMEM((4, 4, 128, 256), BF), VMEM((4, 4, 128, 256), BF),
             VMEM((512, 256), F32), column, column, VMEM((512, 256), BF), VMEM((512, 256), BF), VMEM((128, 1280), F32),
             VMEM((128, 2048), F32), VMEM((128, 2048), F32), VMEM((128, 640), F32),
@@ -836,10 +851,8 @@
     gains = (gain_in, gain_query, gain_key, gain_attn_post, gain_ffn_pre, gain_ffn_post)
     exponents = jnp.arange(0, 256, 2, dtype=F32) / 256
     inverse = 1.0 / ROPE_BASE**exponents
-    angles = positions.astype(F32)[:, None] * inverse[None, :]
-    cos, sin = jnp.cos(angles), jnp.sin(angles)
     layer_out, input_grad, e_full, m_full, l_full = layer(
-        w_query, w_key, w_value, w_out, w_gate, w_up, w_down, *gains, tokens, cotangent, cos, sin
+        w_query, w_key, w_value, w_out, w_gate, w_up, w_down, *gains, tokens, cotangent, positions, inverse.reshape(1, 128)
     )
     layer_out, input_grad, oq, ok, ov, oo, og, ou, od, *gain_grads = unpack(e_full, m_full, l_full, layer_out, input_grad)
     return (layer_out, input_grad, oq, ok, ov, oo, og, ou, od, *[g.reshape(g.shape[1]) for g in gain_grads])

time: 136 us -> 134 us (0.985)
  no operation moved by 1% of the time
where the time goes in v4:
time: 134 us
  Pallas kernels  133 us (99%)
    pallas_call x1, Pallas kernels, layer(): pl.pallas_call(layer_kernel, out_shape=(s(BF, 128, 640), s(F32, 128, 640)...  128 us
    pallas_call x1, Pallas kernels, unpack(): pl.pallas_call(unpack_kernel, out_shape=(jax.ShapeDtypeStruct((128, 640),...  4.76 us

profile of v4, /device:TPU:1, one launch (start us, length us, event | category | flops | bytes accessed | tf_op | source)
XLA Modules:
  0.0 133.9 jit_solution(6556701405605469600)
XLA Ops:
  0.6 0.5 negate_power_fusion.refs_16_
  1.2 127.8 %layer.1 = (bf16[128,640]{1,0:T(8,128)(2,1)}, f32[128,640]{1,0:T(8,128)}, bf16[2,4608,128]{2,1,0:T(8,128)(2,1)}, bf16[2,768,128]{2,1,0:T(8,128)(2,1)}, bf16[2,512,128]{2,1,0:T(8,128)(2,1)}) custom-call(bf16[160,1024]{1,0:T(8,128)(2,1)} %refs_0_.1, bf16[160,256]{1,0:T(8,128)(2,1)} %refs_1_.1, bf16[160,256]{1,0:T(8,128)(2,1)} %refs_2_.1, ...), custom_call_target="tpu_custom_call" | custom-call | tf_op jit(solution)/shard_map/layer/pallas_call | solution.py:776
  128.9 4.8 %unpack.1 = (bf16[128,640]{1,0:T(8,128)(2,1)}, f32[128,640]{1,0:T(8,128)}, f32[160,1024]{1,0:T(8,128)}, f32[160,256]{1,0:T(8,128)}, f32[160,256]{1,0:T(8,128)}, ...) custom-call(bf16[2,4608,128]{2,1,0:T(8,128)(2,1)} %get-tuple-element, ...), custom_call_target="tpu_custom_call" | custom-call | tf_op jit(solution)/shard_map/unpack/pallas_call | solution.py:834

commit v5 on v4

--- a/solution.py
+++ b/solution.py
@@ -340,13 +340,13 @@
 
     wq, wk, wv, wo, wg, wu, wd = take_refs(7)
     gain_ins = take_refs(6)
-    tokens, cot, positions, inverse = take_refs(4)
+    tokens_in, cot_in, positions, inverse = take_refs(4)
     layer_out, input_grad, e_out, m_out, l_full = take_refs(5)
     e_full, m_full = take_refs(2)
     qkv_all, gu, wo_all, wd_all, k_all, v_all = take_refs(6)
     normed, qkvg, attn, projg, ffn, gug, mixed, downg = take_refs(8)
     gain_all, gains, gain_s, gain_other, ge, gm, gl = take_refs(7)
-    cos, sin = take_refs(2)
+    cos, sin, tokens, cot = take_refs(4)
     dk, dv, kin, vin, acc, inv_s, delta_s, do_s, q_s, raw, f_s, g_s, hidden_grad_s = take_refs(13)
     kbufs, vbufs, k2bufs, v2bufs = take_refs(3), take_refs(3), take_refs(3), take_refs(3)
     group_b = [take_refs(9 * len(parts)) for parts in ALL_PARTS]
@@ -361,6 +361,7 @@
             (wg, gu.at[y, :, pl.ds(0, 2048)]), (wu, gu.at[y, :, pl.ds(2048, 2048)]),
             (wq, qkv_all.at[y, :, pl.ds(0, 1024)]), (wk, qkv_all.at[y, :, pl.ds(1024, 256)]),
             (wv, qkv_all.at[y, :, pl.ds(1280, 256)]), (wo, wo_all.at[y]), (wd, wd_all.at[y]),
+            (tokens_in, tokens), (cot_in, cot),
         ]
     ):
         own.append(pltpu.make_async_copy(src, dst, own_sem.at[k]))
@@ -711,24 +712,23 @@
     v2.start()
     middle.step()
     early_b.step()
+    early_a.step()
     k2.end()
     v2.end()
-    early_a.step()
 
     v = raw[:, pl.ds(1024, 256)]
     r = rms(v)
     u = rope_back(kin[z, x].astype(F32), cos[...], sin[...])
-    put_gain(2, gain_grad(v, r, u))
     qkvg[own_rows, pl.ds(1024, 256)] = norm_back(v, r, g_k, u).astype(BF)
     qkvg[own_rows, pl.ds(1280, 256)] = vin[z, x]
     share_kv = net.copy(qkvg.at[own_rows, kv_cols], qkvg.at[other_rows, kv_cols], "c")
+    put_gain(2, gain_grad(v, r, u))
     normed_grad = normed_grad + dot_back(qkvg[own_rows, kv_cols], qkv_all[:, :, kv_cols].reshape(640, 512))
     t = tokens[...].astype(F32)
     r = rms(t)
     put_gain(0, gain_grad(t, r, normed_grad))
     gain_copy = net.copy(gain_s, gain_other, "c")
     input_grad[...] = hidden_grad_s[...] + norm_back(t, r, g_in, normed_grad)
-    middle.step()
     share_kv.wait_recv()
     put(gl, OFF_K, 160, tdot(normed[...], qkvg[:, cols(1024 + c * 128, 128)]), 1)
     put(gl, OFF_V, 160, tdot(normed[...], qkvg[:, cols(1280 + c * 128, 128)]), 1)
@@ -736,6 +736,7 @@
     gl[:, pl.ds(OFF_GAIN, 16), :] = (gain_s[...] + gain_other[...]).astype(BF)
     late = Group(net, gl, l_full, L_PARTS, group_b[3])
     late.step()
+    middle.step()
     early_a.step()
     early_b.step()
     middle.step()
@@ -778,7 +779,7 @@
         out_shape=(
             s(BF, 128, 640), s(F32, 128, 640), s(BF, 2, E_ROWS, 128), s(BF, 2, M_ROWS, 128), s(BF, 2, L_ROWS, 128)
         ),
-        in_specs=[ANYSPEC] * 7 + [VSPEC] * 10,
+        in_specs=[ANYSPEC] * 7 + [VSPEC] * 6 + [ANYSPEC] * 2 + [VSPEC] * 2,
         out_specs=[VSPEC, VSPEC, ANYSPEC, ANYSPEC, VSPEC],
         scratch_shapes=[
             VMEM((2, E_ROWS, 128), BF), VMEM((2, M_ROWS, 128), BF),
@@ -787,7 +788,7 @@
             *[VMEM((256, n), BF) for n in (640, 1536, 1024, 640, 640, 4096, 2048, 640)],
             VMEM((4, 8, 256), F32), VMEM((8, 640), F32), VMEM((4, 16, 128), F32), VMEM((4, 16, 128), F32),
             VMEM((4, E_ROWS, 128), BF), VMEM((4, M_ROWS, 128), BF), VMEM((4, L_ROWS, 128), BF),
-            VMEM((128, 128), F32), VMEM((128, 128), F32),
+            VMEM((128, 128), F32), VMEM((128, 128), F32), VMEM((128, 640), BF), VMEM((128, 640), BF),
             whole, whole, VMEM((4, 4, 128, 256), BF), VMEM((4, 4, 128, 256), BF),
             VMEM((512, 256), F32), column, column, VMEM((512, 256), BF), VMEM((512, 256), BF), VMEM((128, 1280), F32),
             VMEM((128, 2048), F32), VMEM((128, 2048), F32), VMEM((128, 640), F32),
@@ -795,7 +796,7 @@
             *[b for parts in ALL_PARTS for b in group_bufs(parts)],
             pltpu.SemaphoreType.DMA((n,)),
             pltpu.SemaphoreType.DMA((n,)),
-            pltpu.SemaphoreType.DMA((7,)),
+            pltpu.SemaphoreType.DMA((9,)),
         ],
         compiler_params=pltpu.CompilerParams(collective_id=0, has_side_effects=True, vmem_limit_bytes=VMEM_LIMIT),
         name="layer",

time: 134 us -> 133 us (level)
  no operation moved by 1% of the time
where the time goes in v5:
time: 133 us
  Pallas kernels  132 us (99%)
    pallas_call x1, Pallas kernels, layer(): pl.pallas_call(layer_kernel, out_shape=(s(BF, 128, 640), s(F32, 128, 640)...  127 us
    pallas_call x1, Pallas kernels, unpack(): pl.pallas_call(unpack_kernel, out_shape=(jax.ShapeDtypeStruct((128, 640),...  4.76 us

profile of v5, /device:TPU:1, one launch (start us, length us, event | category | flops | bytes accessed | tf_op | source)
XLA Modules:
  0.0 133.2 jit_solution(6146866297698455074)
XLA Ops:
  0.6 0.5 negate_power_fusion.refs_16_
  1.2 127.0 %layer.1 = (bf16[128,640]{1,0:T(8,128)(2,1)}, f32[128,640]{1,0:T(8,128)}, bf16[2,4608,128]{2,1,0:T(8,128)(2,1)}, bf16[2,768,128]{2,1,0:T(8,128)(2,1)}, bf16[2,512,128]{2,1,0:T(8,128)(2,1)}) custom-call(bf16[160,1024]{1,0:T(8,128)(2,1)} %refs_0_.1, bf16[160,256]{1,0:T(8,128)(2,1)} %refs_1_.1, bf16[160,256]{1,0:T(8,128)(2,1)} %refs_2_.1, ...), custom_call_target="tpu_custom_call" | custom-call | tf_op jit(solution)/shard_map/layer/pallas_call | solution.py:777
  128.2 4.8 %unpack.1 = (bf16[128,640]{1,0:T(8,128)(2,1)}, f32[128,640]{1,0:T(8,128)}, f32[160,1024]{1,0:T(8,128)}, f32[160,256]{1,0:T(8,128)}, f32[160,256]{1,0:T(8,128)}, ...) custom-call(bf16[2,4608,128]{2,1,0:T(8,128)(2,1)} %get-tuple-element, ...), custom_call_target="tpu_custom_call" | custom-call | tf_op jit(solution)/shard_map/unpack/pallas_call | solution.py:835
